TPU v7x, 512 devices: a whole 4x8x8 slice. The times are simulated.
512 devices in a mesh: row: 32 (over y_hi, z), col: 16 (over y_lo, x, core).
Axes of the slice: x: 4, y: 8 (y_hi: 4, y_lo: 2; y = y_hi * 2 + y_lo), z: 8, core: 2. Of those that a mesh axis runs over, the one named last changes fastest.
Arguments:
- density: float32 [16, 1024, 1024], P('col', 'row'), may hold values from 0.3 to 3
- velocity: float32 [3, 16, 1024, 1024], P(None, 'col', 'row'), may hold values from -3 to 3
- pressure: float32 [16, 1024, 1024], P('col', 'row'), may hold values from 0.3 to 3
Outputs:
- conserved: float32 [5, 16, 1024, 1024], P(None, None, ('row', 'col'))
All inputs are finite; a program needn't handle non-finite values.
Results may differ from a plain program's by a relative error of at most 0.0003.
Values sent between devices are 32-bit elements; how exact they have to be, the bound alone decides.
No kernel may reach another device: no remote copies, remote signals or barrier semaphores. Data moves between devices by JAX's collectives and lax.ppermute only.
A program may use at most 64 MiB of HBM per device.

v0:
```python
import jax
import jax.numpy as jnp
from jax import lax
from jax.sharding import PartitionSpec as P

RITER = 5


ADIABATIC = 5.0 / 3.0
COURANT_NUMBER = 0.3
PRESSURE_FLOOR = 0.05


def to_fields(density, velocity, pressure):
    moment = density[None] * velocity
    energy = pressure / (ADIABATIC - 1.0) + 0.5 * density * jnp.sum(velocity * velocity, axis=0)
    return jnp.concatenate([density[None], moment, energy[None]], axis=0)


def sweep_line(fields, line_axis, normal, step_size):
    cell_axis = line_axis - 1
    mass_now = fields[0]
    moment = fields[1:4]
    energy = fields[4]
    speeds = moment / mass_now[None]
    press_now = jnp.maximum(
        (ADIABATIC - 1.0) * (energy - 0.5 * mass_now * jnp.sum(speeds * speeds, axis=0)),
        PRESSURE_FLOOR,
    )
    along = speeds[normal - 1]
    sound = jnp.sqrt(ADIABATIC * press_now / mass_now)
    reach = sound * step_size

    def traced(values):
        upper = jnp.roll(values, -1, cell_axis)
        face_value = 7.0 / 12.0 * (values + upper) - 1.0 / 12.0 * (
            jnp.roll(values, 1, cell_axis) + jnp.roll(values, -2, cell_axis)
        )
        face_value = jnp.clip(face_value, jnp.minimum(values, upper), jnp.maximum(values, upper))
        left_edge = jnp.roll(face_value, 1, cell_axis)
        slope = face_value - left_edge
        curve = 6.0 * (values - 0.5 * (left_edge + face_value))
        weight = 1.0 - 2.0 / 3.0 * reach
        from_left = face_value - 0.5 * reach * (slope - weight * curve)
        from_right = jnp.roll(left_edge + 0.5 * reach * (slope + weight * curve), -1, cell_axis)
        return (from_left, from_right)

    mass_left, mass_right = traced(mass_now)
    mass_left = jnp.maximum(mass_left, PRESSURE_FLOOR)
    mass_right = jnp.maximum(mass_right, PRESSURE_FLOOR)
    speed_left, speed_right = traced(along)
    press_left, press_right = traced(press_now)
    press_left = jnp.maximum(press_left, PRESSURE_FLOOR)
    press_right = jnp.maximum(press_right, PRESSURE_FLOOR)
    imped_left = jnp.sqrt(ADIABATIC * press_left * mass_left)
    imped_right = jnp.sqrt(ADIABATIC * press_right * mass_right)
    star_press = (
        imped_right * press_left
        + imped_left * press_right
        + imped_left * imped_right * (speed_left - speed_right)
    ) / (imped_left + imped_right)
    star_press = jnp.maximum(star_press, PRESSURE_FLOOR)
    factor = (ADIABATIC + 1.0) / (2.0 * ADIABATIC)

    def waves(star_press):
        wave_left = imped_left * jnp.sqrt(1.0 + factor * (star_press / press_left - 1.0))
        wave_right = imped_right * jnp.sqrt(1.0 + factor * (star_press / press_right - 1.0))
        star_left = speed_left - (star_press - press_left) / wave_left
        star_right = speed_right + (star_press - press_right) / wave_right
        return (wave_left, wave_right, star_left, star_right)

    for turn in range(RITER):
        wave_left, wave_right, star_left, star_right = waves(star_press)
        slope_left = 2.0 * wave_left**3 / (wave_left * wave_left + imped_left * imped_left)
        slope_right = 2.0 * wave_right**3 / (wave_right * wave_right + imped_right * imped_right)
        star_press = jnp.maximum(
            star_press
            - slope_left * slope_right * (star_right - star_left) / (slope_left + slope_right),
            PRESSURE_FLOOR,
        )
    wave_left, wave_right, star_left, star_right = waves(star_press)
    star_speed = (wave_left * star_left + wave_right * star_right) / (wave_left + wave_right)
    volume = 1.0 + step_size * (star_speed - jnp.roll(star_speed, 1, cell_axis))
    new_along = along - step_size * (star_press - jnp.roll(star_press, 1, cell_axis)) / mass_now
    work_flux = star_press * star_speed
    specific = (
        energy / mass_now - step_size * (work_flux - jnp.roll(work_flux, 1, cell_axis)) / mass_now
    )
    amounts = [mass_now, moment[0], moment[1], moment[2], mass_now * specific]
    amounts[normal] = mass_now * new_along
    amounts = jnp.stack(amounts, axis=0)
    shift = step_size * star_speed
    per_volume = amounts / volume[None]
    donor = jnp.where(shift[None] > 0.0, per_volume, jnp.roll(per_volume, -1, line_axis))
    flux = shift[None] * donor
    return amounts - flux + jnp.roll(flux, 1, line_axis)


def local(density, velocity, pressure):
    sound = jnp.sqrt(ADIABATIC * pressure / density)
    local_speed = jnp.max(jnp.max(jnp.abs(velocity), axis=0) + sound)
    step_size = COURANT_NUMBER / lax.pmax(local_speed, ("row", "col"))
    fields = to_fields(density, velocity, pressure)
    fields = sweep_line(fields, 3, 1, step_size)
    y_lines = lax.all_to_all(fields, "row", split_axis=3, concat_axis=2, tiled=True)
    y_lines = sweep_line(y_lines, 2, 2, step_size)
    fields = lax.all_to_all(y_lines, "row", split_axis=2, concat_axis=3, tiled=True)
    return sweep_line(
        lax.all_to_all(fields, "col", split_axis=2, concat_axis=1, tiled=True), 1, 3, step_size
    )


def solution(mesh):
    placed = (P("col", "row", None), P(None, "col", "row", None), P("col", "row", None))
    return jax.shard_map(
        local,
        mesh=mesh,
        in_specs=placed,
        out_specs=P(None, None, ("row", "col"), None),
        check_vma=False,
    )
```

profile of v0, /device:TPU:1, one launch (start us, length us, event | category | flops | bytes accessed | tf_op | source)
XLA Modules:
  0.0 302.0 jit_solution(12187343027732898358)
XLA Ops:
  0.0 0.8 slice.523
  0.8 0.8 fusion.262
  1.6 1.0 slice.522
  2.6 1.1 fusion.261
  3.7 1.2 multiply_reduce_fusion.1
  5.9 106.1 %pmax.7 = f32[]{:T(128)} all-reduce(f32[]{:T(128)} %fusion.221), channel_id=1, replica_groups=mesh['row'=32,'col'=16] {'row','col'}, use_global_device_ids=true, to_apply=%region_2.0 | all-reduce | flops 1 | bytes 8 | tf_op jit(solution)/shard_map/pmax | solution.py:102
  114.4 1.7 broadcast_compare_fusion
  117.5 1.9 copy.462
  120.0 10.6 %reduce.18 = f32[1024,5,32]{2,1,0:T(8,128)} reduce(f32[1024,5,1,32]{3,2,1,0:T(1,128)S(1)} %bitcast.328, f32[]{:T(128)} %broadcast.4440), dimensions={2}, to_apply=%bitcast.301.reduce_sub_computation | reduce | bytes 1310724
  130.6 3.4 %reshape.9709 = f32[32,1,5120]{2,1,0:T(1,128)S(1)} reshape(f32[1024,5,32]{2,1,0:T(8,128)} %reduce.18) | data formatting | bytes 1310720
  134.0 30.6 %all_to_all.42 = f32[32,1,5120]{2,1,0:T(1,128)S(1)} all-to-all(f32[32,1,5120]{2,1,0:T(1,128)S(1)} %reshape.9709), channel_id=1, replica_groups=mesh['row'=32,'col'=16] {'row'}, dimensions={0} | all-to-all | bytes 1310720 | tf_op jit(solution)/shard_map/all_to_all | solution.py:105
  164.6 2.2 reduce.19
  166.9 4.4 %reshape.9710 = f32[1024,5,1,32]{3,2,1,0:T(1,128)S(1)} reshape(f32[32,5120]{1,0:T(8,128)S(1)} %reduce.19) | data formatting | bytes 1310720
  171.3 1.3 copy.463
  172.6 0.9 all_to_all.32
  173.5 1.2 fusion.240
  174.7 2.3 multiply_reduce_fusion
  177.0 1.6 copy.562
  178.6 0.9 reduce_sum.54
  179.5 0.9 reduce_sum.53
  182.7 0.9 div.2102
  183.6 0.8 slice_bitcast_fusion.63
  185.2 0.9 squeeze.24
  186.1 0.9 slice_bitcast_fusion.65
  187.0 1.5 copy.466
  189.3 0.9 slice_divide_fusion
  201.5 1.6 fusion.238
  207.0 1.2 multiply_subtract_fusion.5
  208.2 1.6 multiply_sqrt_fusion.3
  209.8 1.7 compare_bitcast_fusion.1
  212.8 1.7 copy.495
  214.5 10.6 %reduce.20 = f32[1024,5,32]{2,1,0:T(8,128)} reduce(f32[1024,5,1,32]{3,2,1,0:T(1,128)S(1)} %bitcast.330, f32[]{:T(128)} %broadcast.4440), dimensions={2}, to_apply=%bitcast.303.reduce_sub_computation | reduce | bytes 1310724
  225.1 3.6 %reshape.9711 = f32[32,1,5120]{2,1,0:T(1,128)S(1)} reshape(f32[1024,5,32]{2,1,0:T(8,128)} %reduce.20) | data formatting | bytes 1310720
  228.7 26.3 %all_to_all.43 = f32[32,1,5120]{2,1,0:T(1,128)S(1)} all-to-all(f32[32,1,5120]{2,1,0:T(1,128)S(1)} %reshape.9711), channel_id=1, replica_groups=mesh['row'=32,'col'=16] {'row'}, dimensions={0} | all-to-all | bytes 1310720 | tf_op jit(solution)/shard_map/all_to_all | solution.py:107
  255.0 2.2 reduce.21
  257.2 4.4 %reshape.9712 = f32[1024,5,1,32]{3,2,1,0:T(1,128)S(1)} reshape(f32[32,5120]{1,0:T(8,128)S(1)} %reduce.21) | data formatting | bytes 1310720
  261.6 1.3 copy.496
  263.0 0.9 all_to_all.35
  263.8 2.8 copy.550
  266.7 2.7 reshape.9701
  269.4 16.2 %all_to_all.44 = f32[5,1,32,1024]{3,1,0,2:T(1,128)S(1)} all-to-all(f32[5,1,32,1024]{3,1,0,2:T(1,128)S(1)} %reshape.9701), channel_id=1, replica_groups=mesh['row'=32,'col'=16] {'col'}, dimensions={2} | all-to-all | bytes 1310720 | tf_op jit(solution)/shard_map/all_to_all | solution.py:109
  285.6 0.9 slice_reduce_fusion.4
  286.6 0.9 fusion.3
  291.8 0.8 slice_reduce_fusion.3
  293.0 1.0 multiply_subtract_fusion
  294.8 1.6 fusion.236
  297.6 1.7 compare_bitcast_fusion
  300.2 1.3 copy.546
  (216 shorter events, 31.5 us)
Async XLA Ops:
  0.0 5.1 %copy-start = (f32[1,32,1024]{2,1,0:T(8,128)S(1)}, f32[1,32,1024]{2,1,0:T(8,128)}, u32[]{:S(2)}) copy-start(f32[1,32,1024]{2,1,0:T(8,128)} %param.3) | copy-start | bytes 393220
  0.0 5.1 %copy-start.6 = (f32[1,32,1024]{2,1,0:T(8,128)S(1)}, f32[1,32,1024]{2,1,0:T(8,128)}, u32[]{:S(2)}) copy-start(f32[1,32,1024]{2,1,0:T(8,128)} %param.5) | copy-start | bytes 393220
  177.0 3.4 %copy-start.4 = (f32[1,1,32,32,32]{4,2,3,0,1:T(8,128)S(1)}, f32[1,1,32,32,32]{4,2,3,0,1:T(8,128)}, u32[]{:S(2)}) copy-start(f32[1,1,32,32,32]{4,2,3,0,1:T(8,128)} %get-tuple-element.49) | copy-start | bytes 393220
  181.2 5.8 %copy-start.1 = (f32[3,1,32,32,32]{4,2,3,0,1:T(8,128)S(1)}, f32[3,1,32,32,32]{4,2,3,0,1:T(8,128)}, u32[]{:S(2)}) copy-start(f32[3,1,32,32,32]{4,2,3,0,1:T(8,128)} %get-tuple-element.51) | copy-start | bytes 1179652
  188.5 4.0 %copy-start.7 = (f32[1,1024,32]{1,2,0:T(8,128)S(1)}, f32[1,1024,32]{1,2,0:T(8,128)}, u32[]{:S(2)}) copy-start(f32[1,1024,32]{1,2,0:T(8,128)} %reduce_sum.53) | copy-start | bytes 393220
  188.5 4.0 %copy-start.8 = (f32[1,1022,32]{1,2,0:T(8,128)S(1)}, f32[1,1022,32]{1,2,0:T(8,128)}, u32[]{:S(2)}) copy-start(f32[1,1022,32]{1,2,0:T(8,128)} %get-tuple-element.174) | copy-start | bytes 392452
  188.5 4.0 %copy-start.9 = (f32[1,1024,32]{1,2,0:T(8,128)S(1)}, f32[1,1024,32]{1,2,0:T(8,128)}, u32[]{:S(2)}) copy-start(f32[1,1024,32]{1,2,0:T(8,128)} %squeeze.24) | copy-start | bytes 393220
  188.5 4.0 %copy-start.10 = (f32[1,1023,32]{1,2,0:T(8,128)S(1)}, f32[1,1023,32]{1,2,0:T(8,128)}, u32[]{:S(2)}) copy-start(f32[1,1023,32]{1,2,0:T(8,128)} %get-tuple-element.167) | copy-start | bytes 392836
  188.5 4.0 %copy-start.11 = (f32[1,1023,32]{1,2,0:T(8,128)S(1)}, f32[1,1023,32]{1,2,0:T(8,128)}, u32[]{:S(2)}) copy-start(f32[1,1023,32]{1,2,0:T(8,128)} %get-tuple-element.168) | copy-start | bytes 392836
  188.6 4.0 %copy-start.23 = (f32[1,2,32]{1,2,0:T(8,128)S(1)}, f32[1,2,32]{1,2,0:T(8,128)}, u32[]{:S(2)}) copy-start(f32[1,2,32]{1,2,0:T(8,128)} %get-tuple-element.176) | copy-start | bytes 772
  188.6 4.0 %copy-start.26 = (f32[1,1,32]{1,2,0:T(8,128)S(1)}, f32[1,1,32]{1,2,0:T(8,128)}, u32[]{:S(2)}) copy-start(f32[1,1,32]{1,2,0:T(8,128)} %get-tuple-element.171) | copy-start | bytes 388
  188.6 4.0 %copy-start.27 = (f32[1,1,32]{1,2,0:T(8,128)S(1)}, f32[1,1,32]{1,2,0:T(8,128)}, u32[]{:S(2)}) copy-start(f32[1,1,32]{1,2,0:T(8,128)} %get-tuple-element.172) | copy-start | bytes 388
  197.1 8.1 %copy-start.3 = (f32[1,1,32,32,32]{4,2,3,0,1:T(8,128)S(1)}, f32[1,1,32,32,32]{4,2,3,0,1:T(8,128)}, u32[]{:S(2)}) copy-start(f32[1,1,32,32,32]{4,2,3,0,1:T(8,128)} %get-tuple-element.45) | copy-start | bytes 393220
  197.5 8.6 %copy-start.2 = (f32[1,1,32,32,32]{4,2,3,0,1:T(8,128)S(1)}, f32[1,1,32,32,32]{4,2,3,0,1:T(8,128)}, u32[]{:S(2)}) copy-start(f32[1,1,32,32,32]{4,2,3,0,1:T(8,128)} %get-tuple-element.48) | copy-start | bytes 393220
  201.5 5.4 %copy-start.5 = (f32[1,1,1024,32]{2,3,1,0:T(8,128)S(1)}, f32[1,1,1024,32]{2,3,1,0:T(8,128)}, u32[]{:S(2)}) copy-start(f32[1,1,1024,32]{2,3,1,0:T(8,128)} %reduce_sum.54) | copy-start | bytes 393220
  205.2 2.9 copy-start.12
  205.2 2.9 copy-start.13
  205.2 3.0 copy-start.14
  206.1 3.7 %copy-start.15 = (f32[1,1,1023,32]{2,3,1,0:T(8,128)S(1)}, f32[1,1,1023,32]{2,3,1,0:T(8,128)}, u32[]{:S(2)}) copy-start(f32[1,1,1023,32]{2,3,1,0:T(8,128)} %get-tuple-element.146) | copy-start | bytes 392836
  206.1 3.7 %copy-start.16 = (f32[1,1,1023,32]{2,3,1,0:T(8,128)S(1)}, f32[1,1,1023,32]{2,3,1,0:T(8,128)}, u32[]{:S(2)}) copy-start(f32[1,1,1023,32]{2,3,1,0:T(8,128)} %get-tuple-element.142) | copy-start | bytes 392836
  206.1 3.7 %copy-start.17 = (f32[1,1,1023,32]{2,3,1,0:T(8,128)S(1)}, f32[1,1,1023,32]{2,3,1,0:T(8,128)}, u32[]{:S(2)}) copy-start(f32[1,1,1023,32]{2,3,1,0:T(8,128)} %get-tuple-element.138) | copy-start | bytes 392836
  206.7 3.2 %copy-start.20 = (f32[1,1,1,32]{2,3,1,0:T(8,128)S(1)}, f32[1,1,1,32]{2,3,1,0:T(8,128)}, u32[]{:S(2)}) copy-start(f32[1,1,1,32]{2,3,1,0:T(8,128)} %get-tuple-element.148) | copy-start | bytes 388
  206.7 3.2 %copy-start.21 = (f32[1,1,1,32]{2,3,1,0:T(8,128)S(1)}, f32[1,1,1,32]{2,3,1,0:T(8,128)}, u32[]{:S(2)}) copy-start(f32[1,1,1,32]{2,3,1,0:T(8,128)} %get-tuple-element.144) | copy-start | bytes 388
  206.7 3.2 %copy-start.22 = (f32[1,1,1,32]{2,3,1,0:T(8,128)S(1)}, f32[1,1,1,32]{2,3,1,0:T(8,128)}, u32[]{:S(2)}) copy-start(f32[1,1,1,32]{2,3,1,0:T(8,128)} %get-tuple-element.140) | copy-start | bytes 388
  206.7 4.8 %copy-start.29 = (f32[1,1,1,32]{2,3,1,0:T(8,128)S(1)}, f32[1,1,1,32]{2,3,1,0:T(8,128)}, u32[]{:S(2)}) copy-start(f32[1,1,1,32]{2,3,1,0:T(8,128)} %slice_bitcast_fusion.9) | copy-start | bytes 388
  206.9 4.7 %copy-start.24 = (f32[1,1,1,32]{2,3,1,0:T(8,128)S(1)}, f32[1,1,1,32]{2,3,1,0:T(8,128)}, u32[]{:S(2)}) copy-start(f32[1,1,1,32]{2,3,1,0:T(8,128)} %slice_bitcast_fusion.8) | copy-start | bytes 388
  207.0 4.7 %copy-start.25 = (f32[1,1,1,32]{2,3,1,0:T(8,128)S(1)}, f32[1,1,1,32]{2,3,1,0:T(8,128)}, u32[]{:S(2)}) copy-start(f32[1,1,1,32]{2,3,1,0:T(8,128)} %slice_bitcast_fusion.7) | copy-start | bytes 388
  294.3 2.3 copy-start.28
  294.3 2.3 copy-start.19
  294.3 2.4 copy-start.18
  294.3 2.5 copy-start.30
  294.3 2.5 copy-start.31
  294.3 2.5 copy-start.32
where the time goes:
time: 307 us; the launch traced here: 302 us
  blocking collectives  179 us (58%)
  local copies, waits for them, and re-layouts  71.1 us (23%)
  other arithmetic  49 us (16%)
    pmax x1, blocking collectives, local(): step_size = COURANT_NUMBER / lax.pmax(local_speed, ('row', 'col'))  106 us
    all_to_all x1, blocking collectives, local(): lax.all_to_all(fields, 'row', split_axis=3, concat_axis=2, tiled=True)  30.6 us
    all_to_all x1, blocking collectives, local(): lax.all_to_all(y_lines, 'row', split_axis=2, concat_axis=3, tiled=True)  26.3 us
    unnamed x4, other arithmetic  21.4 us
    unnamed x79, local copies, waits for them, and re-layouts  18.4 us
    all_to_all x1, blocking collectives, local(): lax.all_to_all(fields, 'col', split_axis=2, concat_axis=1, tiled=True)  16.2 us
    all_to_all x4, local copies, waits for them, and re-layouts, local(): lax.all_to_all(y_lines, 'row', split_axis=2, concat_axis=3, tiled=True)  7.73 us

commit v1 on v0

v1 whole, which is shorter than its diff:
```python
import jax
import jax.numpy as jnp
from jax import lax
from jax.experimental import pallas as pl
from jax.experimental.pallas import tpu as pltpu
from jax.sharding import PartitionSpec as P

RITER = 5
ADIABATIC = 5.0 / 3.0
COURANT_NUMBER = 0.3
PRESSURE_FLOOR = 0.05

LINES = 8
LANES = 128
HALO = 4
F32 = jnp.float32


def inverse(value):
    return pl.reciprocal(value, approx=False)


def faces(before, here, after, beyond):
    value = 7.0 / 12.0 * (here + after) - 1.0 / 12.0 * (before + beyond)
    return jnp.minimum(jnp.maximum(value, jnp.minimum(here, after)), jnp.maximum(here, after))


def traced(here, lower, upper, half_reach):
    slope = upper - lower
    curve = 6.0 * here - 3.0 * (lower + upper)
    bend = (1.0 - 4.0 / 3.0 * half_reach) * curve
    return upper - half_reach * (slope - bend), lower + half_reach * (slope + bend)


def riemann(mass_l, speed_l, press_l, mass_r, speed_r, press_r):
    square_l = ADIABATIC * press_l * mass_l
    square_r = ADIABATIC * press_r * mass_r
    gain_l = 0.5 * (ADIABATIC + 1.0) * mass_l
    gain_r = 0.5 * (ADIABATIC + 1.0) * mass_r
    imped_l = square_l * lax.rsqrt(square_l)
    imped_r = square_r * lax.rsqrt(square_r)
    closing = speed_l - speed_r
    star = (imped_r * press_l + imped_l * press_r + imped_l * imped_r * closing) * inverse(imped_l + imped_r)
    star = jnp.maximum(star, PRESSURE_FLOOR)
    for _ in range(RITER):
        jump_l = star - press_l
        jump_r = star - press_r
        root_l = lax.rsqrt(gain_l * jump_l + square_l)
        root_r = lax.rsqrt(gain_r * jump_r + square_r)
        gap = closing - jump_l * root_l - jump_r * root_r
        bottom = root_l * (1.0 + square_l * (root_l * root_l)) + root_r * (1.0 + square_r * (root_r * root_r))
        star = jnp.maximum(star + 2.0 * gap * inverse(bottom), PRESSURE_FLOOR)
    wave_l = gain_l * (star - press_l) + square_l
    wave_r = gain_r * (star - press_r) + square_r
    wave_l = wave_l * lax.rsqrt(wave_l)
    wave_r = wave_r * lax.rsqrt(wave_r)
    speed = (wave_l * speed_l + wave_r * speed_r + (press_l - press_r)) * inverse(wave_l + wave_r)
    return star, speed


def primitives(mass, moments, energy, normal, step):
    thin = inverse(mass)
    square = moments[0] * moments[0] + moments[1] * moments[1] + moments[2] * moments[2]
    press = jnp.maximum((ADIABATIC - 1.0) * (energy - 0.5 * square * thin), PRESSURE_FLOOR)
    sound = ADIABATIC * press * thin
    return moments[normal] * thin, press, 0.5 * step * (sound * lax.rsqrt(sound))


def interfaces(mass, speed, press, half_reach):
    sides = []
    n = mass.shape[0] - 5
    for value in (mass, speed, press):
        face = faces(value[: n + 2], value[1 : n + 3], value[2 : n + 4], value[3 : n + 5])
        up, down = traced(value[2 : n + 3], face[: n + 1], face[1:], half_reach[2 : n + 3])
        sides.append((up[:n], down[1:]))
    (mass_l, mass_r), (speed_l, speed_r), (press_l, press_r) = sides
    return riemann(
        jnp.maximum(mass_l, PRESSURE_FLOOR),
        speed_l,
        jnp.maximum(press_l, PRESSURE_FLOOR),
        jnp.maximum(mass_r, PRESSURE_FLOOR),
        speed_r,
        jnp.maximum(press_r, PRESSURE_FLOOR),
    )


def remap(fields, normal, star, speed, step):
    n = star.shape[0] - 3
    shift = step * speed
    work = shift * star
    thin = inverse(1.0 + (shift[1:] - shift[:-1]))
    push = step * (star[1:] - star[:-1])
    amounts = list(fields)
    amounts[normal] = fields[normal] - push
    amounts[4] = fields[4] - (work[1:] - work[:-1])
    ahead = jnp.maximum(shift[1:-1], 0.0) * thin[:-1]
    back = jnp.minimum(shift[1:-1], 0.0) * thin[1:]
    keep = 1.0 - ahead[1:] + back[:-1]
    return [a[1 : n + 1] * keep + a[:n] * ahead[:-1] - a[2:] * back[1:] for a in amounts]


def shift_up(value):
    lane = lax.broadcasted_iota(jnp.int32, value.shape, value.ndim - 1)
    next_line = pltpu.roll(value, LINES - 1, value.ndim - 2)
    return pltpu.roll(jnp.where(lane == 0, next_line, value), LANES - 1, value.ndim - 1)


def shift_down(value):
    lane = lax.broadcasted_iota(jnp.int32, value.shape, value.ndim - 1)
    last_line = pltpu.roll(value, 1, value.ndim - 2)
    return pltpu.roll(jnp.where(lane == LANES - 1, last_line, value), 1, value.ndim - 1)


def sweep_x(mass, speeds, press, step):
    press = jnp.maximum(press, PRESSURE_FLOOR)
    moments = [mass * v for v in speeds]
    square = speeds[0] * speeds[0] + speeds[1] * speeds[1] + speeds[2] * speeds[2]
    energy = 1.0 / (ADIABATIC - 1.0) * press + 0.5 * mass * square
    sound = ADIABATIC * press * inverse(mass)
    half_reach = 0.5 * step * (sound * lax.rsqrt(sound))
    sides = []
    for value in (mass, speeds[0], press):
        after = shift_up(value)
        face = faces(shift_down(value), value, after, shift_up(after))
        up, down = traced(value, shift_down(face), face, half_reach)
        sides.append((up, shift_up(down)))
    (mass_l, mass_r), (speed_l, speed_r), (press_l, press_r) = sides
    star, speed = riemann(
        jnp.maximum(mass_l, PRESSURE_FLOOR),
        speed_l,
        jnp.maximum(press_l, PRESSURE_FLOOR),
        jnp.maximum(mass_r, PRESSURE_FLOOR),
        speed_r,
        jnp.maximum(press_r, PRESSURE_FLOOR),
    )
    shift = step * speed
    work = shift * star
    thin = inverse(1.0 + (shift - shift_down(shift)))
    push = step * (star - shift_down(star))
    amounts = [mass, moments[0] - push, moments[1], moments[2], energy - (work - shift_down(work))]
    ahead = jnp.maximum(shift, 0.0) * thin
    back = jnp.minimum(shift, 0.0) * shift_up(thin)
    flux = [ahead * a + back * shift_up(a) for a in amounts]
    return [a - f + shift_down(f) for a, f in zip(amounts, flux)]


def row_of(ref, row):
    return ref[pl.ds((row // LINES) * LINES * LINES + row % LINES, LINES, stride=LINES), :]


def survey_kernel(density, velocity, pressure, speed, low, high):
    mass, press = density[...], pressure[...]
    sound = ADIABATIC * press / mass
    largest = jnp.maximum(jnp.abs(velocity[0]), jnp.abs(velocity[1]))
    largest = jnp.maximum(largest, jnp.abs(velocity[2])) + sound * lax.rsqrt(sound)
    speed[0, 0] = jnp.max(largest)
    refs = (density, velocity.at[0], velocity.at[1], velocity.at[2], pressure)
    for index, ref in enumerate(refs):
        for row in range(HALO):
            low[index, row] = row_of(ref, row)
            high[index, row] = row_of(ref, 32 - HALO + row)


X_ROWS = 8
Y_FACES = 7
Y_CELLS = 8


def plane_kernel(top, density, velocity, pressure, below, above, out, raw, fields, prims, star, speed):
    step = COURANT_NUMBER / jnp.full((LINES, LANES), top[0, 0], F32)
    refs = (density, velocity.at[0], velocity.at[1], velocity.at[2], pressure)
    for index, ref in enumerate(refs):
        raw[index, 0:HALO] = below[index]
        raw[index, 32 + HALO : 32 + 2 * HALO] = above[index]
        for row in range(32):
            raw[index, HALO + row] = row_of(ref, row)

    @pl.loop(0, 40 // X_ROWS)
    def _(block):
        rows = pl.ds(block * X_ROWS, X_ROWS)
        got = [raw[index, rows] for index in range(5)]
        new = sweep_x(got[0], got[1:4], got[4], step)
        for index in range(5):
            fields[index, rows] = new[index]
        along, press, half_reach = primitives(new[0], new[1:4], new[4], 1, step)
        prims[0, rows] = along
        prims[1, rows] = press
        prims[2, rows] = half_reach

    @pl.loop(0, 35 // Y_FACES)
    def _(block):
        rows = pl.ds(block * Y_FACES, Y_FACES + 5)
        s, u = interfaces(fields[0, rows], prims[0, rows], prims[1, rows], prims[2, rows])
        star[pl.ds(block * Y_FACES, Y_FACES)] = s
        speed[pl.ds(block * Y_FACES, Y_FACES)] = u

    @pl.loop(0, 32 // Y_CELLS)
    def _(block):
        first = block * Y_CELLS
        rows = pl.ds(first + HALO - 1, Y_CELLS + 2)
        near = pl.ds(first, Y_CELLS + 3)
        new = remap([fields[index, rows] for index in range(5)], 2, star[near], speed[near], step)
        for index in range(5):
            out[pl.ds(block * (Y_CELLS // 2), Y_CELLS // 2), 2 * index : 2 * index + 2] = new[index].reshape(
                Y_CELLS // 2, 2, LINES, LANES
            )


Z_FACES = 8


def column_kernel(top, lines, out, prims, star, speed):
    step = COURANT_NUMBER / jnp.full((LINES, LANES), top[0, 0], F32)

    @pl.loop(0, 2)
    def _(row):
        fields = [lines[:, 2 * index + row] for index in range(5)]
        along, press, half_reach = primitives(fields[0], fields[1:4], fields[4], 2, step)
        for index, value in enumerate((fields[0], along, press, half_reach)):
            prims[index, 2:18] = value
            prims[index, 0:2] = value[14:16]
            prims[index, 18:21] = value[0:3]

        @pl.loop(0, 16 // Z_FACES)
        def _(block):
            cells = pl.ds(block * Z_FACES, Z_FACES + 5)
            s, u = interfaces(*(prims[index, cells] for index in range(4)))
            star[pl.ds(block * Z_FACES, Z_FACES)] = s
            speed[pl.ds(block * Z_FACES, Z_FACES)] = u

        def ring(value, before, after):
            return jnp.concatenate([value[16 - before :], value, value[:after]], axis=0)

        new = remap(
            [ring(f, 1, 1) for f in fields], 3, ring(star[...], 2, 1), ring(speed[...], 2, 1), step
        )
        for index in range(5):
            for z in range(16):
                out[index, z, pl.ds(row, LINES, stride=2), :] = new[index][z]


def tiled(array):
    lead = array.shape[:-2]
    split = array.reshape(lead + (4, LINES, LINES, LANES))
    return jnp.swapaxes(split, -3, -2).reshape(lead + (256, LANES))


def local(density, velocity, pressure, rows, cols):
    vmem = pl.BlockSpec(memory_space=pltpu.VMEM)
    smem = pl.BlockSpec(memory_space=pltpu.SMEM)
    density = tiled(density[0])
    velocity = tiled(velocity[:, 0])
    pressure = tiled(pressure[0])
    halo = jax.ShapeDtypeStruct((5, HALO, LINES, LANES), F32)
    fastest, low, high = pl.pallas_call(
        survey_kernel,
        out_shape=(jax.ShapeDtypeStruct((1, 1), F32), halo, halo),
        in_specs=[vmem] * 3,
        out_specs=(smem, vmem, vmem),
        name="survey",
    )(density, velocity, pressure)
    below = lax.ppermute(high, "row", [(i, (i + 1) % rows) for i in range(rows)])
    above = lax.ppermute(low, "row", [(i, (i - 1) % rows) for i in range(rows)])
    top = lax.pmax(fastest[0, 0], ("row", "col")).reshape(1, 1)
    lines = pl.pallas_call(
        plane_kernel,
        out_shape=jax.ShapeDtypeStruct((16, 10, LINES, LANES), F32),
        in_specs=[smem] + [vmem] * 5,
        out_specs=vmem,
        scratch_shapes=[
            pltpu.VMEM((5, 40, LINES, LANES), F32),
            pltpu.VMEM((5, 40, LINES, LANES), F32),
            pltpu.VMEM((3, 40, LINES, LANES), F32),
            pltpu.VMEM((35, LINES, LANES), F32),
            pltpu.VMEM((35, LINES, LANES), F32),
        ],
        compiler_params=pltpu.CompilerParams(vmem_limit_bytes=32 * 1024 * 1024),
        name="plane_sweeps",
    )(top, density, velocity, pressure, below, above)
    lines = lax.all_to_all(lines, "col", split_axis=0, concat_axis=0, tiled=True)
    result = pl.pallas_call(
        column_kernel,
        out_shape=jax.ShapeDtypeStruct((5, 16, 16, LANES), F32),
        in_specs=[smem, vmem],
        out_specs=vmem,
        scratch_shapes=[
            pltpu.VMEM((4, 21, LINES, LANES), F32),
            pltpu.VMEM((16, LINES, LANES), F32),
            pltpu.VMEM((16, LINES, LANES), F32),
        ],
        compiler_params=pltpu.CompilerParams(vmem_limit_bytes=32 * 1024 * 1024),
        name="column_sweep",
    )(top, lines)
    return jnp.swapaxes(result.reshape(5, 16, LINES, 2, LANES), 2, 3).reshape(5, 16, 2, LINES * LANES)


def solution(mesh):
    rows, cols = mesh.shape["row"], mesh.shape["col"]
    placed = (P("col", "row", None), P(None, "col", "row", None), P("col", "row", None))

    def step(density, velocity, pressure):
        return local(density, velocity, pressure, rows, cols)

    return jax.shard_map(
        step,
        mesh=mesh,
        in_specs=placed,
        out_specs=P(None, None, ("row", "col"), None),
        check_vma=False,
    )
```

time: 307 us -> 140 us (0.46); the launches traced: 302 us -> 140 us
  local copies, waits for them, and re-layouts: 71.1 us -> 0.01 us
  blocking collectives: 179 us -> 111 us
  other arithmetic: 49 us -> 0 us
  starting transfers between devices: 0 us -> 17.1 us
  Pallas kernels: 0 us -> 11.9 us
    all_to_all x3 -> x1, blocking collectives: 73.2 us -> 14.9 us  [local(): lax.all_to_all(lines, 'col', split_axis=0, concat_axis=0, tiled=True)]
    unnamed x4 -> x0, other arithmetic: 21.4 us -> none
    slice x69 -> x0, local copies, waits for them, and re-layouts: 20.4 us -> none  [the longest x18 4.45 us: traced(): jnp.roll(left_edge + 0.5 * reach * (slope + weight * curve), -1, cell_axis)]
    unnamed x79 -> x6, local copies, waits for them, and re-layouts: 18.4 us -> 0.01 us
    ppermute x0 -> x2, starting transfers between devices: none -> 17.1 us  [the longest x1 12.3 us: local(): above = lax.ppermute(low, 'row', [(i, (i - 1) % rows) for i in range(rows)])]
    concatenate x42 -> x0, local copies, waits for them, and re-layouts: 12.3 us -> none  [the longest x12 4.19 us: traced(): left_edge = jnp.roll(face_value, 1, cell_axis)]
    pallas_call x0 -> x3, Pallas kernels: none -> 11.9 us  [the longest x1 6.82 us: local(): pl.pallas_call(plane_kernel, out_shape=jax.ShapeDtypeStruct((16, 10, LINE...]
    pmax x1, blocking collectives: 106 us -> 96 us  [local(): top = lax.pmax(fastest[0, 0], ('row', 'col')).reshape(1, 1)]
  transfers between devices with their start and end apart: 0 -> 2, of which waited for: 0 -> 0; matrix products, arithmetic and copies ran while one was open for 0% -> 0% of each run, Pallas kernels for 0% -> 0%
where the time goes in v1:
time: 140 us
  blocking collectives  111 us (79%)
  starting transfers between devices  17.1 us (12%)
  Pallas kernels  11.9 us (8%)
    pmax x1, blocking collectives, local(): top = lax.pmax(fastest[0, 0], ('row', 'col')).reshape(1, 1)  96 us
    all_to_all x1, blocking collectives, local(): lax.all_to_all(lines, 'col', split_axis=0, concat_axis=0, tiled=True)  14.9 us
    ppermute x1, starting transfers between devices, local(): above = lax.ppermute(low, 'row', [(i, (i - 1) % rows) for i in range(rows)])  12.3 us
    pallas_call x1, Pallas kernels, local(): pl.pallas_call(plane_kernel, out_shape=jax.ShapeDtypeStruct((16, 10, LINE...  6.82 us
    ppermute x1, starting transfers between devices, local(): lax.ppermute(high, 'row', [(i, (i + 1) % rows) for i in range(rows)])  4.83 us
    pallas_call x1, Pallas kernels, local(): pl.pallas_call(column_kernel, out_shape=jax.ShapeDtypeStruct((5, 16, 16,...  3.21 us
  transfers between devices with their start and end apart: 2, of which 0 were waited for; matrix products, arithmetic and copies ran while one was open for 0% of the time, Pallas kernels for 0%

profile of v1, /device:TPU:1, one launch (start us, length us, event | category | flops | bytes accessed | tf_op | source)
XLA Modules:
  0.0 140.1 jit_solution(5376481105388135646)
XLA Ops:
  0.0 0.0 copy-start
  0.0 0.0 copy-start.1
  0.0 0.0 copy-start.2
  0.0 1.9 %survey.1 = (f32[1,1]{1,0:T(1,128)}, f32[5,4,8,128]{3,2,1,0:T(8,128)}, f32[5,4,8,128]{3,2,1,0:T(8,128)}) custom-call(f32[256,128]{1,0:T(8,128)} %bitcast.22, f32[3,256,128]{2,1,0:T(8,128)} %bitcast.20, f32[256,128]{1,0:T(8,128)} %bitcast.24), custom_call_target="tpu_custom_call" | custom-call | tf_op jit(solution)/shard_map/survey/pallas_call | solution.py:255
  1.9 4.8 %collective-permute-start = (f32[5,4,8,128]{3,2,1,0:T(8,128)}, f32[5,4,8,128]{3,2,1,0:T(8,128)S(1)}, u32[]{:S(2)}, u32[]{:S(2)}) collective-permute-start(f32[5,4,8,128]{3,2,1,0:T(8,128)} %get-tuple-element.9), channel_id=1, source_target_pairs={{0,16},{16,32},{32,48},{48,64},{64,80},{80,96},{96,112},{112,128},... | collective-permute-start | bytes 245768 | tf_op jit(solution)/shard_map/ppermute | solution.py:262
  6.7 12.3 %collective-permute-start.1 = (f32[5,4,8,128]{3,2,1,0:T(8,128)}, f32[5,4,8,128]{3,2,1,0:T(8,128)S(1)}, u32[]{:S(2)}, u32[]{:S(2)}) collective-permute-start(f32[5,4,8,128]{3,2,1,0:T(8,128)} %get-tuple-element.10), channel_id=1, source_target_pairs={{0,496},{16,0},{32,16},{48,32},{64,48},{80,64},{96,80},{112,96},{1... | collective-permute-start | bytes 245768 | tf_op jit(solution)/shard_map/ppermute | solution.py:263
  19.0 96.0 %pmax.7.top = f32[1,1]{1,0:T(1,128)} all-reduce(f32[1,1]{1,0:T(1,128)} %get-tuple-element.8), channel_id=1, replica_groups=mesh['row'=32,'col'=16] {'row','col'}, use_global_device_ids=true, to_apply=%region_0.0 | all-reduce | flops 1 | bytes 8 | tf_op jit(solution)/shard_map/pmax | solution.py:264
  115.1 0.0 collective-permute-done.below
  115.1 0.0 collective-permute-done.1.above
  115.1 0.0 copy-done
  115.1 0.0 copy-done.1
  115.1 0.0 copy-done.2
  115.1 6.8 %plane_sweeps.1 = f32[16,10,8,128]{3,2,1,0:T(8,128)S(1)} custom-call(f32[1,1]{1,0:T(1,128)} %pmax.7.top, f32[256,128]{1,0:T(8,128)S(1)} %bitcast.23, f32[3,256,128]{2,1,0:T(8,128)S(1)} %bitcast.21, f32[256,128]{1,0:T(8,128)S(1)} %bitcast.25, f32[5,4,8,128]{3,2,1,0:T(8,128)S(1)} %collective-permute-done.below, f32[5,4,8,128]{3,2,1,0:T(8,128)S(1)} %collective-permute-done.1.above), custom_call_target="tpu_custom_call" | custom-call | tf_op jit(solution)/shard_map/plane_sweeps/pallas_call | solution.py:265
  121.9 14.9 %all_to_all.5.lines = f32[16,10,8,128]{3,2,1,0:T(8,128)S(1)} all-to-all(f32[16,10,8,128]{3,2,1,0:T(8,128)S(1)} %plane_sweeps.1), channel_id=1, replica_groups=mesh['row'=32,'col'=16] {'col'}, dimensions={0} | all-to-all | bytes 1310720 | tf_op jit(solution)/shard_map/all_to_all | solution.py:280
  136.9 3.2 %column_sweep.1 = f32[5,16,16,128]{3,2,1,0:T(8,128)} custom-call(f32[1,1]{1,0:T(1,128)} %pmax.7.top, f32[16,10,8,128]{3,2,1,0:T(8,128)S(1)} %all_to_all.5.lines), custom_call_target="tpu_custom_call" | custom-call | tf_op jit(solution)/shard_map/column_sweep/pallas_call | solution.py:281
Async XLA Ops:
  0.0 115.1 %copy-start = (f32[3,1,32,1024]{3,2,1,0:T(8,128)S(1)}, f32[3,1,32,1024]{3,2,1,0:T(8,128)}, u32[]{:S(2)}) copy-start(f32[3,1,32,1024]{3,2,1,0:T(8,128)} %param.4) | copy-start | bytes 1179652
  0.0 115.1 %copy-start.1 = (f32[1,32,1024]{2,1,0:T(8,128)S(1)}, f32[1,32,1024]{2,1,0:T(8,128)}, u32[]{:S(2)}) copy-start(f32[1,32,1024]{2,1,0:T(8,128)} %param.3) | copy-start | bytes 393220
  0.0 115.1 %copy-start.2 = (f32[1,32,1024]{2,1,0:T(8,128)S(1)}, f32[1,32,1024]{2,1,0:T(8,128)}, u32[]{:S(2)}) copy-start(f32[1,32,1024]{2,1,0:T(8,128)} %param.5) | copy-start | bytes 393220
  1.9 113.2 %collective-permute-start = (f32[5,4,8,128]{3,2,1,0:T(8,128)}, f32[5,4,8,128]{3,2,1,0:T(8,128)S(1)}, u32[]{:S(2)}, u32[]{:S(2)}) collective-permute-start(f32[5,4,8,128]{3,2,1,0:T(8,128)} %get-tuple-element.9), channel_id=1, source_target_pairs={{0,16},{16,32},{32,48},{48,64},{64,80},{80,96},{96,112},{112,128},... | collective-permute-start | bytes 245768 | tf_op jit(solution)/shard_map/ppermute | solution.py:262
  6.7 108.3 %collective-permute-start.1 = (f32[5,4,8,128]{3,2,1,0:T(8,128)}, f32[5,4,8,128]{3,2,1,0:T(8,128)S(1)}, u32[]{:S(2)}, u32[]{:S(2)}) collective-permute-start(f32[5,4,8,128]{3,2,1,0:T(8,128)} %get-tuple-element.10), channel_id=1, source_target_pairs={{0,496},{16,0},{32,16},{48,32},{64,48},{80,64},{96,80},{112,96},{1... | collective-permute-start | bytes 245768 | tf_op jit(solution)/shard_map/ppermute | solution.py:263

commit v2 on v1

--- a/solution.py
+++ b/solution.py
@@ -153,7 +153,7 @@
     sound = ADIABATIC * press / mass
     largest = jnp.maximum(jnp.abs(velocity[0]), jnp.abs(velocity[1]))
     largest = jnp.maximum(largest, jnp.abs(velocity[2])) + sound * lax.rsqrt(sound)
-    speed[0, 0] = jnp.max(largest)
+    speed[...] = jnp.full(speed.shape, jnp.max(largest), F32)
     refs = (density, velocity.at[0], velocity.at[1], velocity.at[2], pressure)
     for index, ref in enumerate(refs):
         for row in range(HALO):
@@ -161,13 +161,21 @@
             high[index, row] = row_of(ref, 32 - HALO + row)
 
 
+def gather_kernel(speeds, speed):
+    speed[...] = jnp.broadcast_to(jnp.max(speeds[...], axis=0, keepdims=True), speed.shape)
+
+
+def step_of(speeds):
+    return COURANT_NUMBER / jnp.broadcast_to(jnp.max(speeds[...], axis=0, keepdims=True), (LINES, LANES))
+
+
 X_ROWS = 8
 Y_FACES = 7
 Y_CELLS = 8
 
 
 def plane_kernel(top, density, velocity, pressure, below, above, out, raw, fields, prims, star, speed):
-    step = COURANT_NUMBER / jnp.full((LINES, LANES), top[0, 0], F32)
+    step = step_of(top)
     refs = (density, velocity.at[0], velocity.at[1], velocity.at[2], pressure)
     for index, ref in enumerate(refs):
         raw[index, 0:HALO] = below[index]
@@ -210,7 +218,7 @@
 
 
 def column_kernel(top, lines, out, prims, star, speed):
-    step = COURANT_NUMBER / jnp.full((LINES, LANES), top[0, 0], F32)
+    step = step_of(top)
 
     @pl.loop(0, 2)
     def _(row):
@@ -245,27 +253,42 @@
     return jnp.swapaxes(split, -3, -2).reshape(lead + (256, LANES))
 
 
-def local(density, velocity, pressure, rows, cols):
+def swap_speeds(speeds, axes):
+    devices = speeds.shape[0]
+    swapped = lax.all_to_all(speeds.reshape(devices, 1, LANES), axes, split_axis=0, concat_axis=0, tiled=True)
+    return swapped.reshape(devices, LANES)
+
+
+def local(density, velocity, pressure, sizes):
     vmem = pl.BlockSpec(memory_space=pltpu.VMEM)
-    smem = pl.BlockSpec(memory_space=pltpu.SMEM)
     density = tiled(density[0])
     velocity = tiled(velocity[:, 0])
     pressure = tiled(pressure[0])
+    near = sizes["x"] * sizes["core"]
+    far = sizes["y_hi"] * sizes["z"] * sizes["y_lo"]
+    rows = sizes["y_hi"] * sizes["z"]
     halo = jax.ShapeDtypeStruct((5, HALO, LINES, LANES), F32)
     fastest, low, high = pl.pallas_call(
         survey_kernel,
-        out_shape=(jax.ShapeDtypeStruct((1, 1), F32), halo, halo),
+        out_shape=(jax.ShapeDtypeStruct((near, LANES), F32), halo, halo),
         in_specs=[vmem] * 3,
-        out_specs=(smem, vmem, vmem),
+        out_specs=(vmem, vmem, vmem),
         name="survey",
     )(density, velocity, pressure)
-    below = lax.ppermute(high, "row", [(i, (i + 1) % rows) for i in range(rows)])
-    above = lax.ppermute(low, "row", [(i, (i - 1) % rows) for i in range(rows)])
-    top = lax.pmax(fastest[0, 0], ("row", "col")).reshape(1, 1)
+    below = lax.ppermute(high, ROW, [(i, (i + 1) % rows) for i in range(rows)])
+    above = lax.ppermute(low, ROW, [(i, (i - 1) % rows) for i in range(rows)])
+    fastest = pl.pallas_call(
+        gather_kernel,
+        out_shape=jax.ShapeDtypeStruct((far, LANES), F32),
+        in_specs=[vmem],
+        out_specs=vmem,
+        name="gather_speeds",
+    )(swap_speeds(fastest, ("x", "core")))
+    top = swap_speeds(fastest, ("y_hi", "z", "y_lo"))
     lines = pl.pallas_call(
         plane_kernel,
         out_shape=jax.ShapeDtypeStruct((16, 10, LINES, LANES), F32),
-        in_specs=[smem] + [vmem] * 5,
+        in_specs=[vmem] * 6,
         out_specs=vmem,
         scratch_shapes=[
             pltpu.VMEM((5, 40, LINES, LANES), F32),
@@ -277,11 +300,11 @@
         compiler_params=pltpu.CompilerParams(vmem_limit_bytes=32 * 1024 * 1024),
         name="plane_sweeps",
     )(top, density, velocity, pressure, below, above)
-    lines = lax.all_to_all(lines, "col", split_axis=0, concat_axis=0, tiled=True)
+    lines = lax.all_to_all(lines, COL, split_axis=0, concat_axis=0, tiled=True)
     result = pl.pallas_call(
         column_kernel,
         out_shape=jax.ShapeDtypeStruct((5, 16, 16, LANES), F32),
-        in_specs=[smem, vmem],
+        in_specs=[vmem, vmem],
         out_specs=vmem,
         scratch_shapes=[
             pltpu.VMEM((4, 21, LINES, LANES), F32),
@@ -294,17 +317,23 @@
     return jnp.swapaxes(result.reshape(5, 16, LINES, 2, LANES), 2, 3).reshape(5, 16, 2, LINES * LANES)
 
 
+ROW = ("y_hi", "z")
+COL = ("y_lo", "x", "core")
+
+
 def solution(mesh):
     rows, cols = mesh.shape["row"], mesh.shape["col"]
-    placed = (P("col", "row", None), P(None, "col", "row", None), P("col", "row", None))
+    sizes = {"y_hi": 4, "z": rows // 4, "y_lo": 2, "x": cols // 4, "core": 2}
+    parts = jax.sharding.Mesh(mesh.devices.reshape(tuple(sizes.values())), ROW + COL)
+    placed = (P(COL, ROW, None), P(None, COL, ROW, None), P(COL, ROW, None))
 
     def step(density, velocity, pressure):
-        return local(density, velocity, pressure, rows, cols)
+        return local(density, velocity, pressure, sizes)
 
     return jax.shard_map(
         step,
-        mesh=mesh,
+        mesh=parts,
         in_specs=placed,
-        out_specs=P(None, None, ("row", "col"), None),
+        out_specs=P(None, None, ROW + COL, None),
         check_vma=False,
     )

time: 140 us -> 73.1 us (0.52)
  blocking collectives: 111 us -> 43.5 us
    pmax x1 -> x0, blocking collectives: 96 us -> none  [local(): top = lax.pmax(fastest[0, 0], ('row', 'col')).reshape(1, 1)]
    all_to_all x1 -> x3, blocking collectives: 14.9 us -> 43.5 us  [the longest x2 27.2 us: swap_speeds(): lax.all_to_all(speeds.reshape(devices, 1, LANES), axes, split_axis=0, con...]
    pallas_call x1 -> x2, Pallas kernels: 1.88 us -> 3.2 us  [the longest x1 1.92 us: local(): pl.pallas_call(survey_kernel, out_shape=(jax.ShapeDtypeStruct((near, LANE...]
  transfers between devices with their start and end apart: 2 -> 2, of which waited for: 0 -> 0; matrix products, arithmetic and copies ran while one was open for 0% -> 0% of each run, Pallas kernels for 0% -> 2%
where the time goes in v2:
time: 73.1 us; the launch traced here: 72.8 us
  blocking collectives  43.5 us (60%)
  starting transfers between devices  17.2 us (24%)
  Pallas kernels  12 us (16%)
    all_to_all x2, blocking collectives, swap_speeds(): lax.all_to_all(speeds.reshape(devices, 1, LANES), axes, split_axis=0, con...  27.2 us
    all_to_all x1, blocking collectives, local(): lines = lax.all_to_all(lines, COL, split_axis=0, concat_axis=0, tiled=True)  16.2 us
    ppermute x1, starting transfers between devices, local(): above = lax.ppermute(low, ROW, [(i, (i - 1) % rows) for i in range(rows)])  12.3 us
    pallas_call x1, Pallas kernels, local(): pl.pallas_call(plane_kernel, out_shape=jax.ShapeDtypeStruct((16, 10, LINE...  6.2 us
    ppermute x1, starting transfers between devices, local(): below = lax.ppermute(high, ROW, [(i, (i + 1) % rows) for i in range(rows)])  4.95 us
    pallas_call x1, Pallas kernels, local(): pl.pallas_call(column_kernel, out_shape=jax.ShapeDtypeStruct((5, 16, 16,...  2.59 us
    pallas_call x1, Pallas kernels, local(): pl.pallas_call(survey_kernel, out_shape=(jax.ShapeDtypeStruct((near, LANE...  1.92 us
  transfers between devices with their start and end apart: 2, of which 0 were waited for; matrix products, arithmetic and copies ran while one was open for 0% of the time, Pallas kernels for 2%

profile of v2, /device:TPU:1, one launch (start us, length us, event | category | flops | bytes accessed | tf_op | source)
XLA Modules:
  0.0 72.8 jit_solution(3123741587120395072)
XLA Ops:
  0.0 0.0 copy-start
  0.0 0.0 copy-start.1
  0.0 0.0 copy-start.2
  0.0 1.9 %survey.1 = (f32[8,128]{1,0:T(8,128)}, f32[5,4,8,128]{3,2,1,0:T(8,128)}, f32[5,4,8,128]{3,2,1,0:T(8,128)}) custom-call(f32[256,128]{1,0:T(8,128)} %bitcast.30, f32[3,256,128]{2,1,0:T(8,128)} %bitcast.28, f32[256,128]{1,0:T(8,128)} %bitcast.32), custom_call_target="tpu_custom_call" | custom-call | tf_op jit(solution)/shard_map/survey/pallas_call | solution.py:271
  1.9 0.0 copy-start.3
  1.9 4.9 %collective-permute-start = (f32[5,4,8,128]{3,2,1,0:T(8,128)}, f32[5,4,8,128]{3,2,1,0:T(8,128)S(1)}, u32[]{:S(2)}, u32[]{:S(2)}) collective-permute-start(f32[5,4,8,128]{3,2,1,0:T(8,128)} %get-tuple-element.9), channel_id=1, source_target_pairs={{0,16},{16,32},{32,48},{48,64},{64,80},{80,96},{96,112},{112,128},... | collective-permute-start | bytes 245768 | tf_op jit(solution)/shard_map/ppermute | solution.py:278
  6.9 12.3 %collective-permute-start.1 = (f32[5,4,8,128]{3,2,1,0:T(8,128)}, f32[5,4,8,128]{3,2,1,0:T(8,128)S(1)}, u32[]{:S(2)}, u32[]{:S(2)}) collective-permute-start(f32[5,4,8,128]{3,2,1,0:T(8,128)} %get-tuple-element.10), channel_id=1, source_target_pairs={{0,496},{16,0},{32,16},{48,32},{64,48},{80,64},{96,80},{112,96},{1... | collective-permute-start | bytes 245768 | tf_op jit(solution)/shard_map/ppermute | solution.py:279
  19.2 0.0 copy-done.3
  19.2 9.7 %all_to_all.15 = f32[8,1,128]{2,1,0:T(1,128)} all-to-all(f32[8,1,128]{2,1,0:T(1,128)S(1)} %bitcast.38), channel_id=1, replica_groups=mesh['y_hi'=4,'z'=8,'y_lo'=2,'x'=4,'core'=2] {'x','core'}, dimensions={0} | all-to-all | bytes 8192 | tf_op jit(solution)/shard_map/all_to_all | solution.py:258
  28.9 1.3 %gather_speeds.1 = f32[64,128]{1,0:T(8,128)} custom-call(f32[8,128]{1,0:T(8,128)} %bitcast.37), custom_call_target="tpu_custom_call" | custom-call | tf_op jit(solution)/shard_map/gather_speeds/pallas_call | solution.py:280
  30.2 17.5 %all_to_all.16 = f32[64,1,128]{2,1,0:T(1,128)S(1)} all-to-all(f32[64,1,128]{2,1,0:T(1,128)} %bitcast.36), channel_id=1, replica_groups=mesh['y_hi'=4,'z'=8,'y_lo'=2,'x'=4,'core'=2] {'y_hi','z','y_lo'}, dimensions={0} | all-to-all | bytes 65536 | tf_op jit(solution)/shard_map/all_to_all | solution.py:258
  47.7 0.0 collective-permute-done.below
  47.7 0.0 collective-permute-done.1.above
  47.7 0.0 copy-done
  47.7 0.0 copy-done.1
  47.7 0.0 copy-done.2
  47.7 6.2 %plane_sweeps.1 = f32[16,10,8,128]{3,2,1,0:T(8,128)S(1)} custom-call(f32[64,128]{1,0:T(8,128)S(1)} %bitcast.34, f32[256,128]{1,0:T(8,128)S(1)} %bitcast.31, f32[3,256,128]{2,1,0:T(8,128)S(1)} %bitcast.29, f32[256,128]{1,0:T(8,128)S(1)} %bitcast.33, f32[5,4,8,128]{3,2,1,0:T(8,128)S(1)} %collective-permute-done.below, ...), custom_call_target="tpu_custom_call" | custom-call | tf_op jit(solution)/shard_map/plane_sweeps/pallas_call | solution.py:288
  53.9 16.2 %all_to_all.17.lines = f32[16,10,8,128]{3,2,1,0:T(8,128)S(1)} all-to-all(f32[16,10,8,128]{3,2,1,0:T(8,128)S(1)} %plane_sweeps.1), channel_id=1, replica_groups=mesh['y_hi'=4,'z'=8,'y_lo'=2,'x'=4,'core'=2] {'y_lo','x','core'}, dimensions={0} | all-to-all | bytes 1310720 | tf_op jit(solution)/shard_map/all_to_all | solution.py:303
  70.2 2.6 %column_sweep.1 = f32[5,16,16,128]{3,2,1,0:T(8,128)} custom-call(f32[64,128]{1,0:T(8,128)S(1)} %bitcast.35, f32[16,10,8,128]{3,2,1,0:T(8,128)S(1)} %all_to_all.17.lines), custom_call_target="tpu_custom_call" | custom-call | tf_op jit(solution)/shard_map/column_sweep/pallas_call | solution.py:304
Async XLA Ops:
  0.0 47.7 %copy-start = (f32[3,1,32,1024]{3,2,1,0:T(8,128)S(1)}, f32[3,1,32,1024]{3,2,1,0:T(8,128)}, u32[]{:S(2)}) copy-start(f32[3,1,32,1024]{3,2,1,0:T(8,128)} %param.4) | copy-start | bytes 1179652
  0.0 47.7 %copy-start.1 = (f32[1,32,1024]{2,1,0:T(8,128)S(1)}, f32[1,32,1024]{2,1,0:T(8,128)}, u32[]{:S(2)}) copy-start(f32[1,32,1024]{2,1,0:T(8,128)} %param.3) | copy-start | bytes 393220
  0.0 47.7 %copy-start.2 = (f32[1,32,1024]{2,1,0:T(8,128)S(1)}, f32[1,32,1024]{2,1,0:T(8,128)}, u32[]{:S(2)}) copy-start(f32[1,32,1024]{2,1,0:T(8,128)} %param.5) | copy-start | bytes 393220
  1.9 17.2 %copy-start.3 = (f32[8,128]{1,0:T(8,128)S(1)}, f32[8,128]{1,0:T(8,128)}, u32[]{:S(2)}) copy-start(f32[8,128]{1,0:T(8,128)} %get-tuple-element.8) | copy-start | bytes 12292
  1.9 45.8 %collective-permute-start = (f32[5,4,8,128]{3,2,1,0:T(8,128)}, f32[5,4,8,128]{3,2,1,0:T(8,128)S(1)}, u32[]{:S(2)}, u32[]{:S(2)}) collective-permute-start(f32[5,4,8,128]{3,2,1,0:T(8,128)} %get-tuple-element.9), channel_id=1, source_target_pairs={{0,16},{16,32},{32,48},{48,64},{64,80},{80,96},{96,112},{112,128},... | collective-permute-start | bytes 245768 | tf_op jit(solution)/shard_map/ppermute | solution.py:278
  6.9 40.8 %collective-permute-start.1 = (f32[5,4,8,128]{3,2,1,0:T(8,128)}, f32[5,4,8,128]{3,2,1,0:T(8,128)S(1)}, u32[]{:S(2)}, u32[]{:S(2)}) collective-permute-start(f32[5,4,8,128]{3,2,1,0:T(8,128)} %get-tuple-element.10), channel_id=1, source_target_pairs={{0,496},{16,0},{32,16},{48,32},{64,48},{80,64},{96,80},{112,96},{1... | collective-permute-start | bytes 245768 | tf_op jit(solution)/shard_map/ppermute | solution.py:279

commit v3 on v2

v3 whole, which is shorter than its diff:
```python
import jax
import jax.numpy as jnp
from jax import lax
from jax.experimental import pallas as pl
from jax.experimental.pallas import tpu as pltpu
from jax.sharding import PartitionSpec as P

RITER = 5
ADIABATIC = 5.0 / 3.0
COURANT_NUMBER = 0.3
PRESSURE_FLOOR = 0.05

LINES = 8
LANES = 128
HALO = 4
ROWS = 32
DEPTH = 16
F32 = jnp.float32


def inverse(value):
    return pl.reciprocal(value, approx=False)


def root(value):
    return value * lax.rsqrt(value)


def faces(before, here, after, beyond):
    value = 7.0 / 12.0 * (here + after) - 1.0 / 12.0 * (before + beyond)
    return jnp.minimum(jnp.maximum(value, jnp.minimum(here, after)), jnp.maximum(here, after))


def parabola(here, lower, upper):
    rise, fall = here - lower, upper - here
    return rise + fall, rise - fall


def reaches(half_reach):
    return half_reach, 3.0 * half_reach - 4.0 * half_reach * half_reach


def riemann(mass_l, speed_l, press_l, mass_r, speed_r, press_r):
    mass_l, mass_r = jnp.maximum(mass_l, PRESSURE_FLOOR), jnp.maximum(mass_r, PRESSURE_FLOOR)
    press_l, press_r = jnp.maximum(press_l, PRESSURE_FLOOR), jnp.maximum(press_r, PRESSURE_FLOOR)
    gain_l = (ADIABATIC + 1.0) / ADIABATIC * inverse(press_l)
    gain_r = (ADIABATIC + 1.0) / ADIABATIC * inverse(press_r)
    light_l = lax.rsqrt(0.5 * ADIABATIC * press_l * mass_l)
    light_r = lax.rsqrt(0.5 * ADIABATIC * press_r * mass_r)
    rest = (ADIABATIC - 1.0) / ADIABATIC
    closing = speed_l - speed_r
    star = (press_l * light_l + press_r * light_r + 2.0**0.5 * closing) * inverse(light_l + light_r)
    star = jnp.maximum(star, PRESSURE_FLOOR)
    for _ in range(RITER):
        root_l = lax.rsqrt(gain_l * star + rest)
        root_r = lax.rsqrt(gain_r * star + rest)
        slow_l = root_l * light_l
        slow_r = root_r * light_r
        gap = closing - (star - press_l) * slow_l - (star - press_r) * slow_r
        bottom = slow_l * (root_l * root_l + 0.5) + slow_r * (root_r * root_r + 0.5)
        star = jnp.maximum(star + gap * inverse(bottom), PRESSURE_FLOOR)
    slow_l = lax.rsqrt(gain_l * star + rest) * light_l
    slow_r = lax.rsqrt(gain_r * star + rest) * light_r
    speed = speed_l * slow_r + speed_r * slow_l + (press_l - press_r) * (slow_l * slow_r)
    return star, speed * inverse(slow_l + slow_r)


def primitives(mass, moments, energy, normal, step):
    thin = inverse(mass)
    square = moments[0] * moments[0] + moments[1] * moments[1] + moments[2] * moments[2]
    press = jnp.maximum((ADIABATIC - 1.0) * (energy - 0.5 * square * thin), PRESSURE_FLOOR)
    return moments[normal] * thin, press, 0.5 * step * root(ADIABATIC * press * thin)


def interfaces(mass, speed, press, half_reach):
    n = mass.shape[0] - 5
    half, bent = reaches(half_reach[2 : n + 3])
    sides = []
    for value in (mass, speed, press):
        face = faces(value[: n + 2], value[1 : n + 3], value[2 : n + 4], value[3 : n + 5])
        lower, upper = face[: n + 1], face[1:]
        slope, curve = parabola(value[2 : n + 3], lower, upper)
        slope, curve = half * slope, bent * curve
        sides.append(((upper - slope + curve)[:n], (lower + slope + curve)[1:]))
    (mass_l, mass_r), (speed_l, speed_r), (press_l, press_r) = sides
    return riemann(mass_l, speed_l, press_l, mass_r, speed_r, press_r)


def remap(fields, normal, star, speed, step):
    n = star.shape[0] - 3
    shift = step * speed
    work = shift * star
    push = step * star
    thin = inverse(1.0 + (shift[1:] - shift[:-1]))
    amounts = list(fields)
    amounts[normal] = fields[normal] - (push[1:] - push[:-1])
    amounts[4] = fields[4] - (work[1:] - work[:-1])
    ahead = jnp.maximum(shift[1:-1], 0.0) * thin[:-1]
    back = jnp.minimum(shift[1:-1], 0.0) * thin[1:]
    keep = 1.0 - ahead[1:] + back[:-1]
    return [a[1 : n + 1] * keep + a[:n] * ahead[:-1] - a[2:] * back[1:] for a in amounts]


def shift_up(value):
    lane = lax.broadcasted_iota(jnp.int32, value.shape, 2)
    turned = pltpu.roll(value, LANES - 1, 2)
    groups = turned.reshape(-1, LINES, LINES, LANES)
    after = jnp.concatenate([groups[:, 1:], groups[:, :1]], axis=1).reshape(value.shape)
    return jnp.where(lane == LANES - 1, after, turned)


def shift_down(value):
    lane = lax.broadcasted_iota(jnp.int32, value.shape, 2)
    turned = pltpu.roll(value, 1, 2)
    groups = turned.reshape(-1, LINES, LINES, LANES)
    before = jnp.concatenate([groups[:, LINES - 1 :], groups[:, : LINES - 1]], axis=1).reshape(value.shape)
    return jnp.where(lane == 0, before, turned)


def prepare(mass, speeds, press):
    press = jnp.maximum(press, PRESSURE_FLOOR)
    square = speeds[0] * speeds[0] + speeds[1] * speeds[1] + speeds[2] * speeds[2]
    energy = 1.0 / (ADIABATIC - 1.0) * press + 0.5 * mass * square
    sound = root(ADIABATIC * press * inverse(mass))
    held = [mass, mass * speeds[0], mass * speeds[1], mass * speeds[2], energy, sound]
    for value in (mass, speeds[0], press):
        after = shift_up(value)
        face = faces(shift_down(value), value, after, shift_up(after))
        held.extend((face,) + parabola(value, shift_down(face), face))
    return held


def solve_x(sound, shapes, step):
    half, bent = reaches(0.5 * step * sound)
    sides = []
    for face, slope, curve in shapes:
        lower = face - slope
        slope, curve = half * slope, bent * curve
        sides.append((face - slope + curve, shift_up(lower + slope + curve)))
    (mass_l, mass_r), (speed_l, speed_r), (press_l, press_r) = sides
    return riemann(mass_l, speed_l, press_l, mass_r, speed_r, press_r)


def remap_x(fields, star, speed, step):
    shift = step * speed
    shift_low, star_low = shift_down(shift), shift_down(star)
    thin = inverse(1.0 + (shift - shift_low))
    amounts = list(fields)
    amounts[1] = fields[1] - step * (star - star_low)
    amounts[4] = fields[4] - (shift * star - shift_low * star_low)
    ahead = jnp.maximum(shift, 0.0) * thin
    back = jnp.minimum(shift, 0.0) * shift_up(thin)
    flux = [ahead * a + back * shift_up(a) for a in amounts]
    return [a - f + shift_down(f) for a, f in zip(amounts, flux)]


def survey_kernel(odd, density, velocity, pressure, speed, paired, other):
    mass, press = density[...], pressure[...]
    sound = ADIABATIC * press / mass
    largest = jnp.maximum(jnp.abs(velocity[0]), jnp.abs(velocity[1]))
    largest = jnp.maximum(largest, jnp.abs(velocity[2])) + root(sound)
    speed[...] = jnp.full(speed.shape, jnp.max(largest), F32)
    refs = (density, velocity.at[0], velocity.at[1], velocity.at[2], pressure)
    for index, ref in enumerate(refs):
        for tile in range(LINES):
            low = ref[pl.ds(tile * LINES, HALO), :]
            high = ref[pl.ds((ROWS - LINES + tile) * LINES + HALO, HALO), :]
            paired[index, tile] = jnp.where(odd[0, 0] == 1, low, high)
            other[0, index, tile] = low
            other[1, index, tile] = high


def step_of(speeds):
    return COURANT_NUMBER / jnp.broadcast_to(jnp.max(speeds[...], axis=0, keepdims=True), (LINES, LANES))


def blocks(total, size):
    return [slice(first, min(first + size, total)) for first in range(0, total, size)]


HELD = 15
Y_FACES = 35
Y_CELLS = 32


def to_lines(ref, tiles, rows):
    for place in range(tiles.shape[0]):
        group, line = rows.start // LINES + place // LINES, place % LINES
        if group < ROWS // LINES:
            ref[pl.ds((group * LINES + HALO) * LINES + line, LINES, stride=LINES), :] = tiles[place]
        else:
            ref[pl.ds(line, HALO, stride=LINES), :] = tiles[place, :HALO]
            ref[pl.ds((ROWS + HALO) * LINES + line, HALO, stride=LINES), :] = tiles[place, HALO:]


def sweep_x(fields, step):
    held = prepare(fields[0], fields[1:4], fields[4])
    star, speed = solve_x(held[5], (held[6:9], held[9:12], held[12:15]), step)
    new = remap_x(held[:5], star, speed, step)
    return new + list(primitives(new[0], new[1:4], new[4], 1, step))


def lines_of(ref, index, rows):
    return ref[index, rows.start * LINES : rows.stop * LINES].reshape(-1, LINES, LANES)


def sweep_y(lines, out, star, speed, step):
    for part in blocks(ROWS + 3, Y_FACES):
        rows = slice(part.start, part.stop + 5)
        star[part], speed[part] = interfaces(*(lines_of(lines, index, rows) for index in (0, 5, 6, 7)))
    for cells in blocks(ROWS, Y_CELLS):
        rows = slice(cells.start + HALO - 1, cells.stop + HALO + 1)
        near = slice(cells.start, cells.stop + 3)
        new = remap([lines_of(lines, index, rows) for index in range(5)], 2, star[near], speed[near], step)
        for index in range(5):
            pairs = new[index].reshape(-1, 2, LINES, LANES)
            out[cells.start // 2 : cells.stop // 2, 2 * index : 2 * index + 2] = pairs


def raw_tiles(density, velocity, pressure):
    refs = (density, velocity.at[0], velocity.at[1], velocity.at[2], pressure)
    return [ref[...].reshape(-1, LINES, LANES) for ref in refs]


def plane_kernel(odd, top, density, velocity, pressure, paired, other, out, rim, lines, star, speed):
    step = step_of(top)
    for index in range(5):
        rim[index, :, :HALO] = jnp.where(odd[0, 0] == 1, paired[index], other[1, index])
        rim[index, :, HALO:] = jnp.where(odd[0, 0] == 1, other[0, index], paired[index])
    inner = raw_tiles(density, velocity, pressure)
    swept = sweep_x([jnp.concatenate([inner[index], rim[index]], axis=0) for index in range(5)], step)
    for index in range(8):
        to_lines(lines.at[index], swept[index], slice(0, ROWS + 2 * HALO))
    sweep_y(lines, out, star, speed, step)


def column_kernel(top, lines, out):
    step = step_of(top)
    for row in range(2):
        fields = [lines[:, 2 * index + row] for index in range(5)]
        along, press, half_reach = primitives(fields[0], fields[1:4], fields[4], 2, step)

        def ring(value, before, after):
            return jnp.concatenate([value[DEPTH - before :], value, value[:after]], axis=0)

        star_now, speed_now = interfaces(*(ring(value, 2, 3) for value in (fields[0], along, press, half_reach)))
        new = remap([ring(f, 1, 1) for f in fields], 3, ring(star_now, 2, 1), ring(speed_now, 2, 1), step)
        for index in range(5):
            for z in range(DEPTH):
                out[index, z, pl.ds(row, LINES, stride=2), :] = new[index][z]


def tiled(array):
    lead = array.shape[:-2]
    split = array.reshape(lead + (ROWS // LINES, LINES, LINES, LANES))
    return jnp.swapaxes(split, -3, -2).reshape(lead + (ROWS * LINES, LANES))


def swap_speeds(speeds, axes):
    order = list(range(speeds.shape[0]))[::-1]
    swapped = lax.all_to_all(speeds, axes, split_axis=0, concat_axis=0, tiled=True, axis_index_groups=[order])
    return swapped.reshape(-1, LANES)


def local(density, velocity, pressure, sizes):
    vmem = pl.BlockSpec(memory_space=pltpu.VMEM)
    smem = pl.BlockSpec(memory_space=pltpu.SMEM)
    wide = pltpu.CompilerParams(vmem_limit_bytes=32 * 1024 * 1024)
    density = tiled(density[0])
    velocity = tiled(velocity[:, 0])
    pressure = tiled(pressure[0])
    near = sizes["x"] * sizes["core"]
    far = sizes["y_hi"] * sizes["z"] * sizes["y_lo"]
    rows = sizes["y_hi"] * sizes["z"]
    halo = jax.ShapeDtypeStruct((5, LINES, HALO, LANES), F32)
    both = jax.ShapeDtypeStruct((2, 5, LINES, HALO, LANES), F32)
    odd = (lax.axis_index("z") % 2).reshape(1, 1)
    fastest, paired, other = pl.pallas_call(
        survey_kernel,
        out_shape=(jax.ShapeDtypeStruct((near * 16, LANES), F32), halo, both),
        in_specs=[smem] + [vmem] * 3,
        out_specs=(vmem, vmem, vmem),
        name="survey",
    )(odd, density, velocity, pressure)
    other = lax.ppermute(other, ROW, [(i, (i + i % 2 * 2 - 1) % rows) for i in range(rows)])
    fastest = swap_speeds(fastest.reshape(near, 16, LANES), ("x", "core"))
    fastest = jnp.broadcast_to(jnp.max(fastest, axis=0, keepdims=True), (far, 2, LANES))
    fastest, paired = lax.optimization_barrier((fastest, paired))
    top = swap_speeds(fastest, ("y_hi", "z", "y_lo"))
    paired = lax.ppermute(paired, ROW, [(i, i ^ 1) for i in range(rows)])
    faces_shape = pltpu.VMEM((ROWS + 3, LINES, LANES), F32)
    rim_shape = pltpu.VMEM((5, LINES, LINES, LANES), F32)
    lines_shape = (8, (ROWS + 2 * HALO) * LINES, LANES)
    sent_shape = jax.ShapeDtypeStruct((DEPTH, 10, LINES, LANES), F32)
    lines = pl.pallas_call(
        plane_kernel,
        out_shape=sent_shape,
        in_specs=[smem] + [vmem] * 6,
        out_specs=vmem,
        scratch_shapes=[rim_shape, pltpu.VMEM(lines_shape, F32), faces_shape, faces_shape],
        compiler_params=wide,
        name="plane_sweeps",
    )(odd, top, density, velocity, pressure, paired, other)
    lines = lax.all_to_all(lines, COL, split_axis=0, concat_axis=0, tiled=True)
    result = pl.pallas_call(
        column_kernel,
        out_shape=jax.ShapeDtypeStruct((5, DEPTH, 2 * LINES, LANES), F32),
        in_specs=[vmem, vmem],
        out_specs=vmem,
        compiler_params=wide,
        name="column_sweep",
    )(top, lines)
    return jnp.swapaxes(result.reshape(5, DEPTH, LINES, 2, LANES), 2, 3).reshape(5, DEPTH, 2, LINES * LANES)


ROW = ("y_hi", "z")
COL = ("y_lo", "x", "core")


def solution(mesh):
    rows, cols = mesh.shape["row"], mesh.shape["col"]
    sizes = {"y_hi": 4, "z": rows // 4, "y_lo": 2, "x": cols // 4, "core": 2}
    parts = jax.sharding.Mesh(mesh.devices.reshape(tuple(sizes.values())), ROW + COL)
    placed = (P(COL, ROW, None), P(None, COL, ROW, None), P(COL, ROW, None))

    def step(density, velocity, pressure):
        return local(density, velocity, pressure, sizes)

    return jax.shard_map(
        step,
        mesh=parts,
        in_specs=placed,
        out_specs=P(None, None, ROW + COL, None),
        check_vma=False,
    )
```

time: 73.1 us -> 60.5 us (0.83)
  blocking collectives: 43.5 us -> 16.3 us
  starting transfers between devices: 17.2 us -> 31.3 us
  Pallas kernels: 12 us -> 8.01 us
  waiting for transfers between devices: 0.01 us -> 3.77 us
    all_to_all x2 -> x0, blocking collectives: 27.2 us -> none  [swap_speeds(): lax.all_to_all(speeds.reshape(devices, 1, LANES), axes, split_axis=0, con...]
    all_to_all x0 -> x2, starting transfers between devices: none -> 17.9 us  [swap_speeds(): lax.all_to_all(speeds, axes, split_axis=0, concat_axis=0, tiled=True, axi...]
    pallas_call x4 -> x3, Pallas kernels: 12 us -> 8.01 us  [the longest x1 3.93 us: local(): pl.pallas_call(plane_kernel, out_shape=sent_shape, in_specs=[smem] + [vme...]
    ppermute x2, starting transfers between devices: 17.2 us -> 13.4 us  [the longest x1 10.4 us: local(): lax.ppermute(other, ROW, [(i, (i + i % 2 * 2 - 1) % rows) for i in range(...]
    ppermute x2, waiting for transfers between devices: 0.01 us -> 2.9 us  [the longest x1 2.9 us: local(): paired = lax.ppermute(paired, ROW, [(i, i ^ 1) for i in range(rows)])]
    all_to_all x0 -> x2, waiting for transfers between devices: none -> 0.87 us  [swap_speeds(): lax.all_to_all(speeds, axes, split_axis=0, concat_axis=0, tiled=True, axi...]
  transfers between devices with their start and end apart: 2 -> 4, of which waited for: 0 -> 2; matrix products, arithmetic and copies ran while one was open for 0% -> 1% of each run, Pallas kernels for 2% -> 0%
where the time goes in v3:
time: 60.5 us; the launch traced here: 60.2 us
  starting transfers between devices  31.3 us (52%)
  blocking collectives  16.3 us (27%)
  Pallas kernels  8.01 us (13%)
  waiting for transfers between devices  3.77 us (6%)
  local copies, waits for them, and re-layouts  0.66 us (1%)
    all_to_all x2, starting transfers between devices, swap_speeds(): lax.all_to_all(speeds, axes, split_axis=0, concat_axis=0, tiled=True, axi...  17.9 us
    all_to_all x1, blocking collectives, local(): lines = lax.all_to_all(lines, COL, split_axis=0, concat_axis=0, tiled=True)  16.3 us
    ppermute x1, starting transfers between devices, local(): lax.ppermute(other, ROW, [(i, (i + i % 2 * 2 - 1) % rows) for i in range(...  10.4 us
    pallas_call x1, Pallas kernels, local(): pl.pallas_call(plane_kernel, out_shape=sent_shape, in_specs=[smem] + [vme...  3.93 us
    ppermute x1, starting transfers between devices, local(): paired = lax.ppermute(paired, ROW, [(i, i ^ 1) for i in range(rows)])  3.08 us
    ppermute x1, waiting for transfers between devices, local(): paired = lax.ppermute(paired, ROW, [(i, i ^ 1) for i in range(rows)])  2.9 us
    pallas_call x1, Pallas kernels, local(): pl.pallas_call(column_kernel, out_shape=jax.ShapeDtypeStruct((5, DEPTH, 2...  2.13 us
    pallas_call x1, Pallas kernels, local(): pl.pallas_call(survey_kernel, out_shape=(jax.ShapeDtypeStruct((near * 16,...  1.94 us
  transfers between devices with their start and end apart: 4, of which 2 were waited for; matrix products, arithmetic and copies ran while one was open for 1% of the time, Pallas kernels for 0%

profile of v3, /device:TPU:1, one launch (start us, length us, event | category | flops | bytes accessed | tf_op | source)
XLA Modules:
  0.0 60.2 jit_solution(3109196771535522051)
XLA Ops:
  0.0 0.0 copy-start
  0.0 1.9 %survey.1 = (f32[128,128]{1,0:T(8,128)}, f32[5,8,4,128]{3,2,1,0:T(4,128)}, f32[2,5,8,4,128]{4,3,2,1,0:T(4,128)}) custom-call(s32[1,1]{1,0:T(1,128)} %bitcast.odd, f32[256,128]{1,0:T(8,128)} %bitcast.27, f32[3,256,128]{2,1,0:T(8,128)} %bitcast.23, f32[256,128]{1,0:T(8,128)} %bitcast.29), custom_call_target="tpu_custom_call" | custom-call | tf_op jit(solution)/shard_map/survey/pallas_call | solution.py:278
  1.9 0.0 copy-start.3
  1.9 10.8 %all-to-all-start = ((f32[8,16,128]{2,1,0:T(8,128)}), f32[8,16,128]{2,1,0:T(8,128)S(1)}, u32[]{:S(2)}, u32[]{:S(2)}) async-start(f32[8,16,128]{2,1,0:T(8,128)} %bitcast.31), calls=%async_computation | async-start | bytes 131072 | tf_op jit(solution)/shard_map/all_to_all | solution.py:261
  12.8 0.0 copy-start.1
  12.8 0.0 copy-start.2
  12.8 10.4 %collective-permute-start.1 = (f32[2,5,8,4,128]{4,3,2,1,0:T(4,128)}, f32[2,5,8,4,128]{4,3,2,1,0:T(4,128)S(1)}, u32[]{:S(2)}, u32[]{:S(2)}) collective-permute-start(f32[2,5,8,4,128]{4,3,2,1,0:T(4,128)} %get-tuple-element.14), channel_id=1, source_target_pairs={{0,496},{16,32},{32,16},{48,64},{64,48},{80,96},{96,80},{112,128},... | collective-permute-start | bytes 491528 | tf_op jit(solution)/shard_map/ppermute | solution.py:285
  23.2 0.0 all-to-all-done
  23.2 0.6 %broadcast_in_dim.2 = f32[64,2,128]{2,1,0:T(2,128)} broadcast(f32[128]{0:T(128)S(1)} %reduce_max.9), dimensions={2} | broadcast | bytes 66048 | tf_op jit(solution)/shard_map/broadcast_in_dim | solution.py:287
  23.9 7.0 %all-to-all-start.1 = ((f32[64,2,128]{2,1,0:T(2,128)}), f32[64,2,128]{2,1,0:T(2,128)S(1)}, u32[]{:S(2)}, u32[]{:S(2)}) async-start(f32[64,2,128]{2,1,0:T(2,128)} %broadcast_in_dim.2), calls=%async_computation.1 | async-start | bytes 131072 | tf_op jit(solution)/shard_map/all_to_all | solution.py:261
  30.9 0.0 copy-done.3
  30.9 3.1 %collective-permute-start = (f32[5,8,4,128]{3,2,1,0:T(4,128)S(1)}, f32[5,8,4,128]{3,2,1,0:T(4,128)S(1)}, u32[]{:S(2)}, u32[]{:S(2)}) collective-permute-start(f32[5,8,4,128]{3,2,1,0:T(4,128)S(1)} %copy-done.3), channel_id=1, source_target_pairs={{0,16},{16,0},{32,48},{48,32},{64,80},{80,64},{96,112},{112,96},{1... | collective-permute-start | bytes 245768 | tf_op jit(solution)/shard_map/ppermute | solution.py:290
  34.0 2.9 %collective-permute-done.paired = f32[5,8,4,128]{3,2,1,0:T(4,128)S(1)} collective-permute-done((f32[5,8,4,128]{3,2,1,0:T(4,128)S(1)}, f32[5,8,4,128]{3,2,1,0:T(4,128)S(1)}, u32[]{:S(2)}, u32[]{:S(2)}) %collective-permute-start) | collective-permute-done | bytes 81952 | tf_op jit(solution)/shard_map/ppermute | solution.py:290
  36.9 0.0 collective-permute-done.1.other
  36.9 0.9 %all-to-all-done.1 = f32[64,2,128]{2,1,0:T(2,128)S(1)} async-done(((f32[64,2,128]{2,1,0:T(2,128)}), f32[64,2,128]{2,1,0:T(2,128)S(1)}, u32[]{:S(2)}, u32[]{:S(2)}) %all-to-all-start.1) | async-done | bytes 65568 | tf_op jit(solution)/shard_map/all_to_all | solution.py:261
  37.8 0.0 copy-done
  37.8 0.0 copy-done.1
  37.8 0.0 copy-done.2
  37.8 3.9 %plane_sweeps.1 = f32[16,10,8,128]{3,2,1,0:T(8,128)S(1)} custom-call(s32[1,1]{1,0:T(1,128)} %bitcast.odd, f32[128,128]{1,0:T(8,128)S(1)} %bitcast.25, f32[256,128]{1,0:T(8,128)S(1)} %bitcast.28, f32[3,256,128]{2,1,0:T(8,128)S(1)} %bitcast.24, f32[256,128]{1,0:T(8,128)S(1)} %bitcast.30, f32[5,8,4,128]{3,2,1,0:T(4,128)S(1)} %collective-permute-done.paired, ...), custom_call_target="tpu_custom_call" | custom-call | tf_op jit(solution)/shard_map/plane_sweeps/pallas_call | solution.py:295
  41.7 16.3 %all_to_all.15.lines = f32[16,10,8,128]{3,2,1,0:T(8,128)S(1)} all-to-all(f32[16,10,8,128]{3,2,1,0:T(8,128)S(1)} %plane_sweeps.1), channel_id=1, replica_groups=mesh['y_hi'=4,'z'=8,'y_lo'=2,'x'=4,'core'=2] {'y_lo','x','core'}, dimensions={0} | all-to-all | bytes 1310720 | tf_op jit(solution)/shard_map/all_to_all | solution.py:304
  58.0 2.1 %column_sweep.1 = f32[5,16,16,128]{3,2,1,0:T(8,128)} custom-call(f32[128,128]{1,0:T(8,128)S(1)} %bitcast.26, f32[16,10,8,128]{3,2,1,0:T(8,128)S(1)} %all_to_all.15.lines), custom_call_target="tpu_custom_call" | custom-call | tf_op jit(solution)/shard_map/column_sweep/pallas_call | solution.py:305
  (1 shorter events, 0.0 us)
Async XLA Ops:
  0.0 37.8 %copy-start = (f32[3,1,32,1024]{3,2,1,0:T(8,128)S(1)}, f32[3,1,32,1024]{3,2,1,0:T(8,128)}, u32[]{:S(2)}) copy-start(f32[3,1,32,1024]{3,2,1,0:T(8,128)} %param.4) | copy-start | bytes 1179652
  1.9 29.0 %copy-start.3 = (f32[5,8,4,128]{3,2,1,0:T(4,128)S(1)}, f32[5,8,4,128]{3,2,1,0:T(4,128)}, u32[]{:S(2)}) copy-start(f32[5,8,4,128]{3,2,1,0:T(4,128)} %get-tuple-element.13) | copy-start | bytes 245764
  1.9 21.2 %all-to-all-start = ((f32[8,16,128]{2,1,0:T(8,128)}), f32[8,16,128]{2,1,0:T(8,128)S(1)}, u32[]{:S(2)}, u32[]{:S(2)}) async-start(f32[8,16,128]{2,1,0:T(8,128)} %bitcast.31), calls=%async_computation | async-start | bytes 131072 | tf_op jit(solution)/shard_map/all_to_all | solution.py:261
  12.8 25.0 %copy-start.1 = (f32[1,32,1024]{2,1,0:T(8,128)S(1)}, f32[1,32,1024]{2,1,0:T(8,128)}, u32[]{:S(2)}) copy-start(f32[1,32,1024]{2,1,0:T(8,128)} %param.3) | copy-start | bytes 393220
  12.8 25.0 %copy-start.2 = (f32[1,32,1024]{2,1,0:T(8,128)S(1)}, f32[1,32,1024]{2,1,0:T(8,128)}, u32[]{:S(2)}) copy-start(f32[1,32,1024]{2,1,0:T(8,128)} %param.5) | copy-start | bytes 393220
  12.8 24.1 %collective-permute-start.1 = (f32[2,5,8,4,128]{4,3,2,1,0:T(4,128)}, f32[2,5,8,4,128]{4,3,2,1,0:T(4,128)S(1)}, u32[]{:S(2)}, u32[]{:S(2)}) collective-permute-start(f32[2,5,8,4,128]{4,3,2,1,0:T(4,128)} %get-tuple-element.14), channel_id=1, source_target_pairs={{0,496},{16,32},{32,16},{48,64},{64,48},{80,96},{96,80},{112,128},... | collective-permute-start | bytes 491528 | tf_op jit(solution)/shard_map/ppermute | solution.py:285
  23.9 13.9 %all-to-all-start.1 = ((f32[64,2,128]{2,1,0:T(2,128)}), f32[64,2,128]{2,1,0:T(2,128)S(1)}, u32[]{:S(2)}, u32[]{:S(2)}) async-start(f32[64,2,128]{2,1,0:T(2,128)} %broadcast_in_dim.2), calls=%async_computation.1 | async-start | bytes 131072 | tf_op jit(solution)/shard_map/all_to_all | solution.py:261
  30.9 6.0 %collective-permute-start = (f32[5,8,4,128]{3,2,1,0:T(4,128)S(1)}, f32[5,8,4,128]{3,2,1,0:T(4,128)S(1)}, u32[]{:S(2)}, u32[]{:S(2)}) collective-permute-start(f32[5,8,4,128]{3,2,1,0:T(4,128)S(1)} %copy-done.3), channel_id=1, source_target_pairs={{0,16},{16,0},{32,48},{48,32},{64,80},{80,64},{96,112},{112,96},{1... | collective-permute-start | bytes 245768 | tf_op jit(solution)/shard_map/ppermute | solution.py:290

commit v4 on v3

--- a/solution.py
+++ b/solution.py
@@ -193,11 +193,14 @@
             ref[pl.ds((ROWS + HALO) * LINES + line, HALO, stride=LINES), :] = tiles[place, HALO:]
 
 
-def sweep_x(fields, step):
-    held = prepare(fields[0], fields[1:4], fields[4])
+def sweep_x(held, step):
     star, speed = solve_x(held[5], (held[6:9], held[9:12], held[12:15]), step)
     new = remap_x(held[:5], star, speed, step)
     return new + list(primitives(new[0], new[1:4], new[4], 1, step))
+
+
+def seat(column):
+    return column ^ 4
 
 
 def lines_of(ref, index, rows):
@@ -214,7 +217,8 @@
         new = remap([lines_of(lines, index, rows) for index in range(5)], 2, star[near], speed[near], step)
         for index in range(5):
             pairs = new[index].reshape(-1, 2, LINES, LANES)
-            out[cells.start // 2 : cells.stop // 2, 2 * index : 2 * index + 2] = pairs
+            for pair in range(pairs.shape[0]):
+                out[seat(cells.start // 2 + pair), 2 * index : 2 * index + 2] = pairs[pair]
 
 
 def raw_tiles(density, velocity, pressure):
@@ -222,13 +226,19 @@
     return [ref[...].reshape(-1, LINES, LANES) for ref in refs]
 
 
-def plane_kernel(odd, top, density, velocity, pressure, paired, other, out, rim, lines, star, speed):
+def prepare_kernel(density, velocity, pressure, held):
+    inner = raw_tiles(density, velocity, pressure)
+    for index, value in enumerate(prepare(inner[0], inner[1:4], inner[4])):
+        held[index] = value
+
+
+def plane_kernel(odd, top, held, paired, other, out, rim, lines, star, speed):
     step = step_of(top)
     for index in range(5):
         rim[index, :, :HALO] = jnp.where(odd[0, 0] == 1, paired[index], other[1, index])
         rim[index, :, HALO:] = jnp.where(odd[0, 0] == 1, other[0, index], paired[index])
-    inner = raw_tiles(density, velocity, pressure)
-    swept = sweep_x([jnp.concatenate([inner[index], rim[index]], axis=0) for index in range(5)], step)
+    outer = prepare(rim[0], [rim[1], rim[2], rim[3]], rim[4])
+    swept = sweep_x([jnp.concatenate([held[index], outer[index]], axis=0) for index in range(HELD)], step)
     for index in range(8):
         to_lines(lines.at[index], swept[index], slice(0, ROWS + 2 * HALO))
     sweep_y(lines, out, star, speed, step)
@@ -237,7 +247,7 @@
 def column_kernel(top, lines, out):
     step = step_of(top)
     for row in range(2):
-        fields = [lines[:, 2 * index + row] for index in range(5)]
+        fields = [jnp.stack([lines[seat(z), 2 * index + row] for z in range(DEPTH)]) for index in range(5)]
         along, press, half_reach = primitives(fields[0], fields[1:4], fields[4], 2, step)
 
         def ring(value, before, after):
@@ -274,7 +284,7 @@
     rows = sizes["y_hi"] * sizes["z"]
     halo = jax.ShapeDtypeStruct((5, LINES, HALO, LANES), F32)
     both = jax.ShapeDtypeStruct((2, 5, LINES, HALO, LANES), F32)
-    odd = (lax.axis_index("z") % 2).reshape(1, 1)
+    odd = (lax.axis_index("z") & 1).reshape(1, 1)
     fastest, paired, other = pl.pallas_call(
         survey_kernel,
         out_shape=(jax.ShapeDtypeStruct((near * 16, LANES), F32), halo, both),
@@ -285,9 +295,18 @@
     other = lax.ppermute(other, ROW, [(i, (i + i % 2 * 2 - 1) % rows) for i in range(rows)])
     fastest = swap_speeds(fastest.reshape(near, 16, LANES), ("x", "core"))
     fastest = jnp.broadcast_to(jnp.max(fastest, axis=0, keepdims=True), (far, 2, LANES))
-    fastest, paired = lax.optimization_barrier((fastest, paired))
+    fastest, paired, density, velocity, pressure = lax.optimization_barrier((fastest, paired, density, velocity, pressure))
     top = swap_speeds(fastest, ("y_hi", "z", "y_lo"))
     paired = lax.ppermute(paired, ROW, [(i, i ^ 1) for i in range(rows)])
+    held = pl.pallas_call(
+        prepare_kernel,
+        out_shape=jax.ShapeDtypeStruct((HELD, ROWS, LINES, LANES), F32),
+        in_specs=[vmem] * 3,
+        out_specs=vmem,
+        compiler_params=pltpu.CompilerParams(vmem_limit_bytes=32 * 1024 * 1024),
+        cost_estimate=pl.CostEstimate(flops=4000000, bytes_accessed=2600000, transcendentals=100000),
+        name="prepare_rows",
+    )(density, velocity, pressure)
     faces_shape = pltpu.VMEM((ROWS + 3, LINES, LANES), F32)
     rim_shape = pltpu.VMEM((5, LINES, LINES, LANES), F32)
     lines_shape = (8, (ROWS + 2 * HALO) * LINES, LANES)
@@ -295,13 +314,14 @@
     lines = pl.pallas_call(
         plane_kernel,
         out_shape=sent_shape,
-        in_specs=[smem] + [vmem] * 6,
+        in_specs=[smem] + [vmem] * 4,
         out_specs=vmem,
         scratch_shapes=[rim_shape, pltpu.VMEM(lines_shape, F32), faces_shape, faces_shape],
         compiler_params=wide,
         name="plane_sweeps",
-    )(odd, top, density, velocity, pressure, paired, other)
-    lines = lax.all_to_all(lines, COL, split_axis=0, concat_axis=0, tiled=True)
+    )(odd, top, held, paired, other)
+    seats = [seat(column) for column in range(DEPTH)]
+    lines = lax.all_to_all(lines, COL, split_axis=0, concat_axis=0, tiled=True, axis_index_groups=[seats])
     result = pl.pallas_call(
         column_kernel,
         out_shape=jax.ShapeDtypeStruct((5, DEPTH, 2 * LINES, LANES), F32),

time: 60.5 us -> 59.1 us (0.977)
  waiting for transfers between devices: 3.77 us -> 0.32 us
  local copies, waits for them, and re-layouts: 0.66 us -> 3.45 us
    ppermute x1, waiting for transfers between devices: 2.9 us -> 0.01 us  [local(): paired = lax.ppermute(paired, ROW, [(i, i ^ 1) for i in range(rows)])]
    unnamed x8 -> x6, local copies, waits for them, and re-layouts: 0.01 us -> 2.8 us
    pallas_call x0 -> x1, Pallas kernels: none -> 0.63 us  [local(): pl.pallas_call(prepare_kernel, out_shape=jax.ShapeDtypeStruct((HELD, ROWS...]
  transfers between devices with their start and end apart: 4 -> 4, of which waited for: 2 -> 1; matrix products, arithmetic and copies ran while one was open for 1% -> 1% of each run, Pallas kernels for 0% -> 1%
where the time goes in v4:
time: 59.1 us; the launch traced here: 58.7 us
  starting transfers between devices  31.1 us (53%)
  blocking collectives  15.8 us (27%)
  Pallas kernels  8.02 us (14%)
  local copies, waits for them, and re-layouts  3.45 us (6%)
    all_to_all x2, starting transfers between devices, swap_speeds(): lax.all_to_all(speeds, axes, split_axis=0, concat_axis=0, tiled=True, axi...  17.8 us
    all_to_all x1, blocking collectives, local(): lax.all_to_all(lines, COL, split_axis=0, concat_axis=0, tiled=True, axis_...  15.8 us
    ppermute x1, starting transfers between devices, local(): lax.ppermute(other, ROW, [(i, (i + i % 2 * 2 - 1) % rows) for i in range(...  10.2 us
    pallas_call x1, Pallas kernels, local(): pl.pallas_call(plane_kernel, out_shape=sent_shape, in_specs=[smem] + [vme...  3.35 us
    ppermute x1, starting transfers between devices, local(): paired = lax.ppermute(paired, ROW, [(i, i ^ 1) for i in range(rows)])  3.08 us
    unnamed x6, local copies, waits for them, and re-layouts  2.8 us
    pallas_call x1, Pallas kernels, local(): pl.pallas_call(column_kernel, out_shape=jax.ShapeDtypeStruct((5, DEPTH, 2...  2.13 us
    pallas_call x1, Pallas kernels, local(): pl.pallas_call(survey_kernel, out_shape=(jax.ShapeDtypeStruct((near * 16,...  1.9 us
  transfers between devices with their start and end apart: 4, of which 1 were waited for; matrix products, arithmetic and copies ran while one was open for 1% of the time, Pallas kernels for 1%

profile of v4, /device:TPU:1, one launch (start us, length us, event | category | flops | bytes accessed | tf_op | source)
XLA Modules:
  0.0 58.7 jit_solution(8918456988198873855)
XLA Ops:
  0.0 1.9 %survey.1 = (f32[128,128]{1,0:T(8,128)}, f32[5,8,4,128]{3,2,1,0:T(4,128)}, f32[2,5,8,4,128]{4,3,2,1,0:T(4,128)}) custom-call(s32[1,1]{1,0:T(1,128)} %bitcast.odd, f32[256,128]{1,0:T(8,128)} %bitcast.27, f32[3,256,128]{2,1,0:T(8,128)} %bitcast.23, f32[256,128]{1,0:T(8,128)} %bitcast.29), custom_call_target="tpu_custom_call" | custom-call | tf_op jit(solution)/shard_map/survey/pallas_call | solution.py:288
  1.9 10.7 %all-to-all-start = ((f32[8,16,128]{2,1,0:T(8,128)}), f32[8,16,128]{2,1,0:T(8,128)S(1)}, u32[]{:S(2)}, u32[]{:S(2)}) async-start(f32[8,16,128]{2,1,0:T(8,128)} %bitcast.31), calls=%async_computation | async-start | bytes 131072 | tf_op jit(solution)/shard_map/all_to_all | solution.py:271
  12.6 10.2 %collective-permute-start.1 = (f32[2,5,8,4,128]{4,3,2,1,0:T(4,128)}, f32[2,5,8,4,128]{4,3,2,1,0:T(4,128)S(1)}, u32[]{:S(2)}, u32[]{:S(2)}) collective-permute-start(f32[2,5,8,4,128]{4,3,2,1,0:T(4,128)} %get-tuple-element.20), channel_id=1, source_target_pairs={{0,496},{16,32},{32,16},{48,64},{64,48},{80,96},{96,80},{112,128},... | collective-permute-start | bytes 491528 | tf_op jit(solution)/shard_map/ppermute | solution.py:295
  22.8 0.0 all-to-all-done
  22.9 0.7 %broadcast_in_dim.2 = f32[64,2,128]{2,1,0:T(2,128)} broadcast(f32[128]{0:T(128)S(1)} %reduce_max.9), dimensions={2} | broadcast | bytes 66048 | tf_op jit(solution)/shard_map/broadcast_in_dim | solution.py:297
  23.5 7.0 %all-to-all-start.1 = ((f32[64,2,128]{2,1,0:T(2,128)}), f32[64,2,128]{2,1,0:T(2,128)S(1)}, u32[]{:S(2)}, u32[]{:S(2)}) async-start(f32[64,2,128]{2,1,0:T(2,128)} %broadcast_in_dim.2), calls=%async_computation.1 | async-start | bytes 131072 | tf_op jit(solution)/shard_map/all_to_all | solution.py:271
  30.6 3.1 %collective-permute-start = (f32[5,8,4,128]{3,2,1,0:T(4,128)}, f32[5,8,4,128]{3,2,1,0:T(4,128)S(1)}, u32[]{:S(2)}, u32[]{:S(2)}) collective-permute-start(f32[5,8,4,128]{3,2,1,0:T(4,128)} %get-tuple-element.19), channel_id=1, source_target_pairs={{0,16},{16,0},{32,48},{48,32},{64,80},{80,64},{96,112},{112,96},{1... | collective-permute-start | bytes 245768 | tf_op jit(solution)/shard_map/ppermute | solution.py:300
  33.7 0.0 copy-start
  33.7 1.0 %copy-done = f32[3,1,32,1024]{3,2,1,0:T(8,128)S(1)} copy-done((f32[3,1,32,1024]{3,2,1,0:T(8,128)S(1)}, f32[3,1,32,1024]{3,2,1,0:T(8,128)}, u32[]{:S(2)}) %copy-start) | copy-done | bytes 393240
  34.7 0.0 copy-start.1
  34.7 0.9 %copy-done.1 = f32[1,32,1024]{2,1,0:T(8,128)S(1)} copy-done((f32[1,32,1024]{2,1,0:T(8,128)S(1)}, f32[1,32,1024]{2,1,0:T(8,128)}, u32[]{:S(2)}) %copy-start.1) | copy-done | bytes 131096
  35.6 0.0 copy-start.2
  35.6 0.9 %copy-done.2 = f32[1,32,1024]{2,1,0:T(8,128)S(1)} copy-done((f32[1,32,1024]{2,1,0:T(8,128)S(1)}, f32[1,32,1024]{2,1,0:T(8,128)}, u32[]{:S(2)}) %copy-start.2) | copy-done | bytes 131096
  36.5 0.6 %prepare_rows.1.held = f32[15,32,8,128]{3,2,1,0:T(8,128)S(1)} custom-call(f32[256,128]{1,0:T(8,128)S(1)} %bitcast.28, f32[3,256,128]{2,1,0:T(8,128)S(1)} %bitcast.24, f32[256,128]{1,0:T(8,128)S(1)} %bitcast.30), custom_call_target="tpu_custom_call" | custom-call | flops 4000000 | bytes 2600000 | tf_op jit(solution)/shard_map/prepare_rows/pallas_call | solution.py:301
  37.1 0.0 collective-permute-done.paired
  37.1 0.0 collective-permute-done.1.other
  37.1 0.3 all-to-all-done.1
  37.5 3.4 %plane_sweeps.1 = f32[16,10,8,128]{3,2,1,0:T(8,128)S(1)} custom-call(s32[1,1]{1,0:T(1,128)} %bitcast.odd, f32[128,128]{1,0:T(8,128)S(1)} %bitcast.25, f32[15,32,8,128]{3,2,1,0:T(8,128)S(1)} %prepare_rows.1.held, f32[5,8,4,128]{3,2,1,0:T(4,128)S(1)} %collective-permute-done.paired, f32[2,5,8,4,128]{4,3,2,1,0:T(4,128)S(1)} %collective-permute-done.1.other), custom_call_target="tpu_custom_call" | custom-call | tf_op jit(solution)/shard_map/plane_sweeps/pallas_call | solution.py:314
  40.8 15.8 %all_to_all.15.lines = f32[16,10,8,128]{3,2,1,0:T(8,128)S(1)} all-to-all(f32[16,10,8,128]{3,2,1,0:T(8,128)S(1)} %plane_sweeps.1), channel_id=1, replica_groups={{4,5,6,7,0,1,2,3,12,13,14,15,8,9,10,11},{20,21,22,23,16,17,18,19,28,29,..., dimensions={0} | all-to-all | bytes 1310720 | tf_op jit(solution)/shard_map/all_to_all | solution.py:324
  56.6 2.1 %column_sweep.1 = f32[5,16,16,128]{3,2,1,0:T(8,128)} custom-call(f32[128,128]{1,0:T(8,128)S(1)} %bitcast.26, f32[16,10,8,128]{3,2,1,0:T(8,128)S(1)} %all_to_all.15.lines), custom_call_target="tpu_custom_call" | custom-call | tf_op jit(solution)/shard_map/column_sweep/pallas_call | solution.py:325
  (1 shorter events, 0.0 us)
Async XLA Ops:
  1.9 20.9 %all-to-all-start = ((f32[8,16,128]{2,1,0:T(8,128)}), f32[8,16,128]{2,1,0:T(8,128)S(1)}, u32[]{:S(2)}, u32[]{:S(2)}) async-start(f32[8,16,128]{2,1,0:T(8,128)} %bitcast.31), calls=%async_computation | async-start | bytes 131072 | tf_op jit(solution)/shard_map/all_to_all | solution.py:271
  12.6 24.5 %collective-permute-start.1 = (f32[2,5,8,4,128]{4,3,2,1,0:T(4,128)}, f32[2,5,8,4,128]{4,3,2,1,0:T(4,128)S(1)}, u32[]{:S(2)}, u32[]{:S(2)}) collective-permute-start(f32[2,5,8,4,128]{4,3,2,1,0:T(4,128)} %get-tuple-element.20), channel_id=1, source_target_pairs={{0,496},{16,32},{32,16},{48,64},{64,48},{80,96},{96,80},{112,128},... | collective-permute-start | bytes 491528 | tf_op jit(solution)/shard_map/ppermute | solution.py:295
  23.5 13.9 %all-to-all-start.1 = ((f32[64,2,128]{2,1,0:T(2,128)}), f32[64,2,128]{2,1,0:T(2,128)S(1)}, u32[]{:S(2)}, u32[]{:S(2)}) async-start(f32[64,2,128]{2,1,0:T(2,128)} %broadcast_in_dim.2), calls=%async_computation.1 | async-start | bytes 131072 | tf_op jit(solution)/shard_map/all_to_all | solution.py:271
  30.6 6.5 %collective-permute-start = (f32[5,8,4,128]{3,2,1,0:T(4,128)}, f32[5,8,4,128]{3,2,1,0:T(4,128)S(1)}, u32[]{:S(2)}, u32[]{:S(2)}) collective-permute-start(f32[5,8,4,128]{3,2,1,0:T(4,128)} %get-tuple-element.19), channel_id=1, source_target_pairs={{0,16},{16,0},{32,48},{48,32},{64,80},{80,64},{96,112},{112,96},{1... | collective-permute-start | bytes 245768 | tf_op jit(solution)/shard_map/ppermute | solution.py:300
  33.7 1.0 %copy-start = (f32[3,1,32,1024]{3,2,1,0:T(8,128)S(1)}, f32[3,1,32,1024]{3,2,1,0:T(8,128)}, u32[]{:S(2)}) copy-start(f32[3,1,32,1024]{3,2,1,0:T(8,128)} %param.4) | copy-start | bytes 1179652
  34.7 0.9 %copy-start.1 = (f32[1,32,1024]{2,1,0:T(8,128)S(1)}, f32[1,32,1024]{2,1,0:T(8,128)}, u32[]{:S(2)}) copy-start(f32[1,32,1024]{2,1,0:T(8,128)} %param.3) | copy-start | bytes 393220
  35.6 0.9 %copy-start.2 = (f32[1,32,1024]{2,1,0:T(8,128)S(1)}, f32[1,32,1024]{2,1,0:T(8,128)}, u32[]{:S(2)}) copy-start(f32[1,32,1024]{2,1,0:T(8,128)} %param.5) | copy-start | bytes 393220

commit v5 on v4

--- a/solution.py
+++ b/solution.py
@@ -166,8 +166,7 @@
             low = ref[pl.ds(tile * LINES, HALO), :]
             high = ref[pl.ds((ROWS - LINES + tile) * LINES + HALO, HALO), :]
             paired[index, tile] = jnp.where(odd[0, 0] == 1, low, high)
-            other[0, index, tile] = low
-            other[1, index, tile] = high
+            other[index, tile] = jnp.where(odd[0, 0] == 1, high, low)
 
 
 def step_of(speeds):
@@ -235,8 +234,8 @@
 def plane_kernel(odd, top, held, paired, other, out, rim, lines, star, speed):
     step = step_of(top)
     for index in range(5):
-        rim[index, :, :HALO] = jnp.where(odd[0, 0] == 1, paired[index], other[1, index])
-        rim[index, :, HALO:] = jnp.where(odd[0, 0] == 1, other[0, index], paired[index])
+        rim[index, :, :HALO] = jnp.where(odd[0, 0] == 1, paired[index], other[index])
+        rim[index, :, HALO:] = jnp.where(odd[0, 0] == 1, other[index], paired[index])
     outer = prepare(rim[0], [rim[1], rim[2], rim[3]], rim[4])
     swept = sweep_x([jnp.concatenate([held[index], outer[index]], axis=0) for index in range(HELD)], step)
     for index in range(8):
@@ -283,21 +282,20 @@
     far = sizes["y_hi"] * sizes["z"] * sizes["y_lo"]
     rows = sizes["y_hi"] * sizes["z"]
     halo = jax.ShapeDtypeStruct((5, LINES, HALO, LANES), F32)
-    both = jax.ShapeDtypeStruct((2, 5, LINES, HALO, LANES), F32)
     odd = (lax.axis_index("z") & 1).reshape(1, 1)
     fastest, paired, other = pl.pallas_call(
         survey_kernel,
-        out_shape=(jax.ShapeDtypeStruct((near * 16, LANES), F32), halo, both),
+        out_shape=(jax.ShapeDtypeStruct((far * 2, LANES), F32), halo, halo),
         in_specs=[smem] + [vmem] * 3,
         out_specs=(vmem, vmem, vmem),
         name="survey",
     )(odd, density, velocity, pressure)
     other = lax.ppermute(other, ROW, [(i, (i + i % 2 * 2 - 1) % rows) for i in range(rows)])
-    fastest = swap_speeds(fastest.reshape(near, 16, LANES), ("x", "core"))
-    fastest = jnp.broadcast_to(jnp.max(fastest, axis=0, keepdims=True), (far, 2, LANES))
-    fastest, paired, density, velocity, pressure = lax.optimization_barrier((fastest, paired, density, velocity, pressure))
-    top = swap_speeds(fastest, ("y_hi", "z", "y_lo"))
     paired = lax.ppermute(paired, ROW, [(i, i ^ 1) for i in range(rows)])
+    fastest = swap_speeds(fastest.reshape(far, 2, LANES), ("y_hi", "z", "y_lo"))
+    fastest = jnp.broadcast_to(jnp.max(fastest, axis=0, keepdims=True), (near, 1, LANES))
+    fastest, density, velocity, pressure = lax.optimization_barrier((fastest, density, velocity, pressure))
+    top = swap_speeds(fastest, ("x", "core"))
     held = pl.pallas_call(
         prepare_kernel,
         out_shape=jax.ShapeDtypeStruct((HELD, ROWS, LINES, LANES), F32),

time: 59.1 us -> 57 us (0.964)
  blocking collectives: 15.8 us -> 14.2 us
  starting transfers between devices: 31.1 us -> 29.7 us
  waiting for transfers between devices: 0.32 us -> 0.98 us
    ppermute x1, starting transfers between devices: 10.2 us -> 2.79 us  [local(): lax.ppermute(other, ROW, [(i, (i + i % 2 * 2 - 1) % rows) for i in range(...]
    all_to_all x2, starting transfers between devices: 17.8 us -> 23.9 us  [swap_speeds(): lax.all_to_all(speeds, axes, split_axis=0, concat_axis=0, tiled=True, axi...]
    all_to_all x1, blocking collectives: 15.8 us -> 14.2 us  [local(): lax.all_to_all(lines, COL, split_axis=0, concat_axis=0, tiled=True, axis_...]
    all_to_all x2, waiting for transfers between devices: 0.31 us -> 0.98 us  [swap_speeds(): lax.all_to_all(speeds, axes, split_axis=0, concat_axis=0, tiled=True, axi...]
where the time goes in v5:
time: 57 us; the launch traced here: 56.6 us
  starting transfers between devices  29.7 us (52%)
  blocking collectives  14.2 us (25%)
  Pallas kernels  8.12 us (14%)
  local copies, waits for them, and re-layouts  3.4 us (6%)
  waiting for transfers between devices  0.98 us (2%)
    all_to_all x2, starting transfers between devices, swap_speeds(): lax.all_to_all(speeds, axes, split_axis=0, concat_axis=0, tiled=True, axi...  23.9 us
    all_to_all x1, blocking collectives, local(): lax.all_to_all(lines, COL, split_axis=0, concat_axis=0, tiled=True, axis_...  14.2 us
    pallas_call x1, Pallas kernels, local(): pl.pallas_call(plane_kernel, out_shape=sent_shape, in_specs=[smem] + [vme...  3.45 us
    ppermute x1, starting transfers between devices, local(): paired = lax.ppermute(paired, ROW, [(i, i ^ 1) for i in range(rows)])  3.08 us
    unnamed x6, local copies, waits for them, and re-layouts  2.8 us
    ppermute x1, starting transfers between devices, local(): lax.ppermute(other, ROW, [(i, (i + i % 2 * 2 - 1) % rows) for i in range(...  2.79 us
    pallas_call x1, Pallas kernels, local(): pl.pallas_call(column_kernel, out_shape=jax.ShapeDtypeStruct((5, DEPTH, 2...  2.14 us
    pallas_call x1, Pallas kernels, local(): pl.pallas_call(survey_kernel, out_shape=(jax.ShapeDtypeStruct((far * 2, L...  1.9 us
  transfers between devices with their start and end apart: 4, of which 1 were waited for; matrix products, arithmetic and copies ran while one was open for 1% of the time, Pallas kernels for 1%

profile of v5, /device:TPU:1, one launch (start us, length us, event | category | flops | bytes accessed | tf_op | source)
XLA Modules:
  0.0 56.6 jit_solution(1229953904732780764)
XLA Ops:
  0.0 1.9 %survey.1 = (f32[128,128]{1,0:T(8,128)}, f32[5,8,4,128]{3,2,1,0:T(4,128)}, f32[5,8,4,128]{3,2,1,0:T(4,128)}) custom-call(s32[1,1]{1,0:T(1,128)} %bitcast.odd, f32[256,128]{1,0:T(8,128)} %bitcast.25, f32[3,256,128]{2,1,0:T(8,128)} %bitcast.23, f32[256,128]{1,0:T(8,128)} %bitcast.27), custom_call_target="tpu_custom_call" | custom-call | tf_op jit(solution)/shard_map/survey/pallas_call | solution.py:286
  1.9 17.3 %all-to-all-start = ((f32[64,2,128]{2,1,0:T(2,128)}), f32[64,2,128]{2,1,0:T(2,128)S(1)}, u32[]{:S(2)}, u32[]{:S(2)}) async-start(f32[64,2,128]{2,1,0:T(2,128)} %bitcast.31), calls=%async_computation | async-start | bytes 131072 | tf_op jit(solution)/shard_map/all_to_all | solution.py:270
  19.2 3.1 %collective-permute-start = (f32[5,8,4,128]{3,2,1,0:T(4,128)}, f32[5,8,4,128]{3,2,1,0:T(4,128)S(1)}, u32[]{:S(2)}, u32[]{:S(2)}) collective-permute-start(f32[5,8,4,128]{3,2,1,0:T(4,128)} %get-tuple-element.17), channel_id=1, source_target_pairs={{0,16},{16,0},{32,48},{48,32},{64,80},{80,64},{96,112},{112,96},{1... | collective-permute-start | bytes 245768 | tf_op jit(solution)/shard_map/ppermute | solution.py:294
  22.3 2.8 %collective-permute-start.1 = (f32[5,8,4,128]{3,2,1,0:T(4,128)}, f32[5,8,4,128]{3,2,1,0:T(4,128)S(1)}, u32[]{:S(2)}, u32[]{:S(2)}) collective-permute-start(f32[5,8,4,128]{3,2,1,0:T(4,128)} %get-tuple-element.18), channel_id=1, source_target_pairs={{0,496},{16,32},{32,16},{48,64},{64,48},{80,96},{96,80},{112,128},... | collective-permute-start | bytes 245768 | tf_op jit(solution)/shard_map/ppermute | solution.py:293
  25.1 1.0 %all-to-all-done = f32[64,2,128]{2,1,0:T(2,128)S(1)} async-done(((f32[64,2,128]{2,1,0:T(2,128)}), f32[64,2,128]{2,1,0:T(2,128)S(1)}, u32[]{:S(2)}, u32[]{:S(2)}) %all-to-all-start) | async-done | bytes 65568 | tf_op jit(solution)/shard_map/all_to_all | solution.py:270
  26.0 0.1 reduce_max.9
  26.1 0.6 %broadcast_in_dim.4 = f32[8,1,128]{2,1,0:T(1,128)} broadcast(f32[128]{0:T(128)S(1)} %reduce_max.9), dimensions={2} | broadcast | bytes 4608 | tf_op jit(solution)/shard_map/broadcast_in_dim | solution.py:296
  26.7 6.6 %all-to-all-start.1 = ((f32[8,1,128]{2,1,0:T(1,128)}), f32[8,1,128]{2,1,0:T(1,128)S(1)}, u32[]{:S(2)}, u32[]{:S(2)}) async-start(f32[8,1,128]{2,1,0:T(1,128)} %broadcast_in_dim.4), calls=%async_computation.1 | async-start | bytes 8192 | tf_op jit(solution)/shard_map/all_to_all | solution.py:270
  33.3 0.0 copy-start
  33.3 1.0 %copy-done = f32[3,1,32,1024]{3,2,1,0:T(8,128)S(1)} copy-done((f32[3,1,32,1024]{3,2,1,0:T(8,128)S(1)}, f32[3,1,32,1024]{3,2,1,0:T(8,128)}, u32[]{:S(2)}) %copy-start) | copy-done | bytes 393240
  34.3 0.0 copy-start.1
  34.3 0.9 %copy-done.1 = f32[1,32,1024]{2,1,0:T(8,128)S(1)} copy-done((f32[1,32,1024]{2,1,0:T(8,128)S(1)}, f32[1,32,1024]{2,1,0:T(8,128)}, u32[]{:S(2)}) %copy-start.1) | copy-done | bytes 131096
  35.2 0.0 copy-start.2
  35.2 0.9 %copy-done.2 = f32[1,32,1024]{2,1,0:T(8,128)S(1)} copy-done((f32[1,32,1024]{2,1,0:T(8,128)S(1)}, f32[1,32,1024]{2,1,0:T(8,128)}, u32[]{:S(2)}) %copy-start.2) | copy-done | bytes 131096
  36.1 0.6 %prepare_rows.1.held = f32[15,32,8,128]{3,2,1,0:T(8,128)S(1)} custom-call(f32[256,128]{1,0:T(8,128)S(1)} %bitcast.26, f32[3,256,128]{2,1,0:T(8,128)S(1)} %bitcast.24, f32[256,128]{1,0:T(8,128)S(1)} %bitcast.28), custom_call_target="tpu_custom_call" | custom-call | flops 4000000 | bytes 2600000 | tf_op jit(solution)/shard_map/prepare_rows/pallas_call | solution.py:299
  36.8 0.0 collective-permute-done.paired
  36.8 0.0 collective-permute-done.1.other
  36.8 0.0 all-to-all-done.1
  36.8 3.4 %plane_sweeps.1 = f32[16,10,8,128]{3,2,1,0:T(8,128)S(1)} custom-call(s32[1,1]{1,0:T(1,128)} %bitcast.odd, f32[8,128]{1,0:T(8,128)S(1)} %bitcast.29, f32[15,32,8,128]{3,2,1,0:T(8,128)S(1)} %prepare_rows.1.held, f32[5,8,4,128]{3,2,1,0:T(4,128)S(1)} %collective-permute-done.paired, f32[5,8,4,128]{3,2,1,0:T(4,128)S(1)} %collective-permute-done.1.other), custom_call_target="tpu_custom_call" | custom-call | tf_op jit(solution)/shard_map/plane_sweeps/pallas_call | solution.py:312
  40.3 14.2 %all_to_all.15.lines = f32[16,10,8,128]{3,2,1,0:T(8,128)S(1)} all-to-all(f32[16,10,8,128]{3,2,1,0:T(8,128)S(1)} %plane_sweeps.1), channel_id=1, replica_groups={{4,5,6,7,0,1,2,3,12,13,14,15,8,9,10,11},{20,21,22,23,16,17,18,19,28,29,..., dimensions={0} | all-to-all | bytes 1310720 | tf_op jit(solution)/shard_map/all_to_all | solution.py:322
  54.5 2.1 %column_sweep.1 = f32[5,16,16,128]{3,2,1,0:T(8,128)} custom-call(f32[8,128]{1,0:T(8,128)S(1)} %bitcast.30, f32[16,10,8,128]{3,2,1,0:T(8,128)S(1)} %all_to_all.15.lines), custom_call_target="tpu_custom_call" | custom-call | tf_op jit(solution)/shard_map/column_sweep/pallas_call | solution.py:323
Async XLA Ops:
  1.9 24.1 %all-to-all-start = ((f32[64,2,128]{2,1,0:T(2,128)}), f32[64,2,128]{2,1,0:T(2,128)S(1)}, u32[]{:S(2)}, u32[]{:S(2)}) async-start(f32[64,2,128]{2,1,0:T(2,128)} %bitcast.31), calls=%async_computation | async-start | bytes 131072 | tf_op jit(solution)/shard_map/all_to_all | solution.py:270
  19.2 17.6 %collective-permute-start = (f32[5,8,4,128]{3,2,1,0:T(4,128)}, f32[5,8,4,128]{3,2,1,0:T(4,128)S(1)}, u32[]{:S(2)}, u32[]{:S(2)}) collective-permute-start(f32[5,8,4,128]{3,2,1,0:T(4,128)} %get-tuple-element.17), channel_id=1, source_target_pairs={{0,16},{16,0},{32,48},{48,32},{64,80},{80,64},{96,112},{112,96},{1... | collective-permute-start | bytes 245768 | tf_op jit(solution)/shard_map/ppermute | solution.py:294
  22.3 14.5 %collective-permute-start.1 = (f32[5,8,4,128]{3,2,1,0:T(4,128)}, f32[5,8,4,128]{3,2,1,0:T(4,128)S(1)}, u32[]{:S(2)}, u32[]{:S(2)}) collective-permute-start(f32[5,8,4,128]{3,2,1,0:T(4,128)} %get-tuple-element.18), channel_id=1, source_target_pairs={{0,496},{16,32},{32,16},{48,64},{64,48},{80,96},{96,80},{112,128},... | collective-permute-start | bytes 245768 | tf_op jit(solution)/shard_map/ppermute | solution.py:293
  26.7 10.1 %all-to-all-start.1 = ((f32[8,1,128]{2,1,0:T(1,128)}), f32[8,1,128]{2,1,0:T(1,128)S(1)}, u32[]{:S(2)}, u32[]{:S(2)}) async-start(f32[8,1,128]{2,1,0:T(1,128)} %broadcast_in_dim.4), calls=%async_computation.1 | async-start | bytes 8192 | tf_op jit(solution)/shard_map/all_to_all | solution.py:270
  33.3 1.0 %copy-start = (f32[3,1,32,1024]{3,2,1,0:T(8,128)S(1)}, f32[3,1,32,1024]{3,2,1,0:T(8,128)}, u32[]{:S(2)}) copy-start(f32[3,1,32,1024]{3,2,1,0:T(8,128)} %param.4) | copy-start | bytes 1179652
  34.3 0.9 %copy-start.1 = (f32[1,32,1024]{2,1,0:T(8,128)S(1)}, f32[1,32,1024]{2,1,0:T(8,128)}, u32[]{:S(2)}) copy-start(f32[1,32,1024]{2,1,0:T(8,128)} %param.3) | copy-start | bytes 393220
  35.2 0.9 %copy-start.2 = (f32[1,32,1024]{2,1,0:T(8,128)S(1)}, f32[1,32,1024]{2,1,0:T(8,128)}, u32[]{:S(2)}) copy-start(f32[1,32,1024]{2,1,0:T(8,128)} %param.5) | copy-start | bytes 393220

commit v6 on v5

--- a/solution.py
+++ b/solution.py
@@ -154,12 +154,14 @@
     return [a - f + shift_down(f) for a, f in zip(amounts, flux)]
 
 
-def survey_kernel(odd, density, velocity, pressure, speed, paired, other):
+def survey_kernel(odd, density, velocity, pressure, speed, paired, other, kept):
     mass, press = density[...], pressure[...]
     sound = ADIABATIC * press / mass
     largest = jnp.maximum(jnp.abs(velocity[0]), jnp.abs(velocity[1]))
     largest = jnp.maximum(largest, jnp.abs(velocity[2])) + root(sound)
     speed[...] = jnp.full(speed.shape, jnp.max(largest), F32)
+    for index, value in enumerate(raw_tiles(density, velocity, pressure)):
+        kept[index] = value
     refs = (density, velocity.at[0], velocity.at[1], velocity.at[2], pressure)
     for index, ref in enumerate(refs):
         for tile in range(LINES):
@@ -199,7 +201,7 @@
 
 
 def seat(column):
-    return column ^ 4
+    return column ^ 13
 
 
 def lines_of(ref, index, rows):
@@ -225,9 +227,8 @@
     return [ref[...].reshape(-1, LINES, LANES) for ref in refs]
 
 
-def prepare_kernel(density, velocity, pressure, held):
-    inner = raw_tiles(density, velocity, pressure)
-    for index, value in enumerate(prepare(inner[0], inner[1:4], inner[4])):
+def prepare_kernel(arrived, kept, held):
+    for index, value in enumerate(prepare(kept[0], [kept[1], kept[2], kept[3]], kept[4])):
         held[index] = value
 
 
@@ -281,30 +282,31 @@
     near = sizes["x"] * sizes["core"]
     far = sizes["y_hi"] * sizes["z"] * sizes["y_lo"]
     rows = sizes["y_hi"] * sizes["z"]
+    kept_shape = pltpu.VMEM((5, ROWS, LINES, LANES), F32)
     halo = jax.ShapeDtypeStruct((5, LINES, HALO, LANES), F32)
     odd = (lax.axis_index("z") & 1).reshape(1, 1)
-    fastest, paired, other = pl.pallas_call(
+    fastest, paired, other, kept = pl.pallas_call(
         survey_kernel,
-        out_shape=(jax.ShapeDtypeStruct((far * 2, LANES), F32), halo, halo),
+        out_shape=(jax.ShapeDtypeStruct((far * 2, LANES), F32), halo, halo, kept_shape),
         in_specs=[smem] + [vmem] * 3,
-        out_specs=(vmem, vmem, vmem),
+        out_specs=(vmem, vmem, vmem, vmem),
         name="survey",
     )(odd, density, velocity, pressure)
     other = lax.ppermute(other, ROW, [(i, (i + i % 2 * 2 - 1) % rows) for i in range(rows)])
     paired = lax.ppermute(paired, ROW, [(i, i ^ 1) for i in range(rows)])
     fastest = swap_speeds(fastest.reshape(far, 2, LANES), ("y_hi", "z", "y_lo"))
     fastest = jnp.broadcast_to(jnp.max(fastest, axis=0, keepdims=True), (near, 1, LANES))
-    fastest, density, velocity, pressure = lax.optimization_barrier((fastest, density, velocity, pressure))
-    top = swap_speeds(fastest, ("x", "core"))
     held = pl.pallas_call(
         prepare_kernel,
         out_shape=jax.ShapeDtypeStruct((HELD, ROWS, LINES, LANES), F32),
-        in_specs=[vmem] * 3,
+        in_specs=[pl.BlockSpec(memory_space=pl.ANY), vmem],
         out_specs=vmem,
-        compiler_params=pltpu.CompilerParams(vmem_limit_bytes=32 * 1024 * 1024),
+        compiler_params=wide,
         cost_estimate=pl.CostEstimate(flops=4000000, bytes_accessed=2600000, transcendentals=100000),
         name="prepare_rows",
-    )(density, velocity, pressure)
+    )(paired, kept)
+    fastest, held = lax.optimization_barrier((fastest, held))
+    top = swap_speeds(fastest, ("x", "core"))
     faces_shape = pltpu.VMEM((ROWS + 3, LINES, LANES), F32)
     rim_shape = pltpu.VMEM((5, LINES, LINES, LANES), F32)
     lines_shape = (8, (ROWS + 2 * HALO) * LINES, LANES)

time: 57 us -> 56.1 us (0.984)
  local copies, waits for them, and re-layouts: 3.4 us -> 0.6 us
  waiting for transfers between devices: 0.98 us -> 3.18 us
    unnamed x6 -> x0, local copies, waits for them, and re-layouts: 2.8 us -> none
    all_to_all x2, waiting for transfers between devices: 0.98 us -> 2.93 us  [swap_speeds(): lax.all_to_all(speeds, axes, split_axis=0, concat_axis=0, tiled=True, axi...]
  transfers between devices with their start and end apart: 4 -> 4, of which waited for: 1 -> 3; matrix products, arithmetic and copies ran while one was open for 1% -> 1% of each run, Pallas kernels for 1% -> 1%
where the time goes in v6:
time: 56.1 us; the launch traced here: 55.8 us
  starting transfers between devices  29.7 us (53%)
  blocking collectives  14.1 us (25%)
  Pallas kernels  8.02 us (14%)
  waiting for transfers between devices  3.18 us (6%)
  local copies, waits for them, and re-layouts  0.6 us (1%)
    all_to_all x2, starting transfers between devices, swap_speeds(): lax.all_to_all(speeds, axes, split_axis=0, concat_axis=0, tiled=True, axi...  23.9 us
    all_to_all x1, blocking collectives, local(): lax.all_to_all(lines, COL, split_axis=0, concat_axis=0, tiled=True, axis_...  14.1 us
    pallas_call x1, Pallas kernels, local(): pl.pallas_call(plane_kernel, out_shape=sent_shape, in_specs=[smem] + [vme...  3.36 us
    ppermute x1, starting transfers between devices, local(): paired = lax.ppermute(paired, ROW, [(i, i ^ 1) for i in range(rows)])  3.08 us
    all_to_all x2, waiting for transfers between devices, swap_speeds(): lax.all_to_all(speeds, axes, split_axis=0, concat_axis=0, tiled=True, axi...  2.93 us
    ppermute x1, starting transfers between devices, local(): lax.ppermute(other, ROW, [(i, (i + i % 2 * 2 - 1) % rows) for i in range(...  2.79 us
    pallas_call x1, Pallas kernels, local(): pl.pallas_call(column_kernel, out_shape=jax.ShapeDtypeStruct((5, DEPTH, 2...  2.14 us
    pallas_call x1, Pallas kernels, local(): pl.pallas_call(survey_kernel, out_shape=(jax.ShapeDtypeStruct((far * 2, L...  1.89 us
  transfers between devices with their start and end apart: 4, of which 3 were waited for; matrix products, arithmetic and copies ran while one was open for 1% of the time, Pallas kernels for 1%

profile of v6, /device:TPU:1, one launch (start us, length us, event | category | flops | bytes accessed | tf_op | source)
XLA Modules:
  0.0 55.8 jit_solution(4117299958757652192)
XLA Ops:
  0.0 1.9 %survey.1 = (f32[128,128]{1,0:T(8,128)}, f32[5,8,4,128]{3,2,1,0:T(4,128)}, f32[5,8,4,128]{3,2,1,0:T(4,128)}, f32[5,32,8,128]{3,2,1,0:T(8,128)S(1)}) custom-call(s32[1,1]{1,0:T(1,128)} %bitcast.odd, f32[256,128]{1,0:T(8,128)} %bitcast.26, f32[3,256,128]{2,1,0:T(8,128)} %bitcast.25, f32[256,128]{1,0:T(8,128)} %bitcast.27), custom_call_target="tpu_custom_call" | custom-call | tf_op jit(solution)/shard_map/survey/pallas_call | solution.py:288
  1.9 17.3 %all-to-all-start = ((f32[64,2,128]{2,1,0:T(2,128)}), f32[64,2,128]{2,1,0:T(2,128)S(1)}, u32[]{:S(2)}, u32[]{:S(2)}) async-start(f32[64,2,128]{2,1,0:T(2,128)} %bitcast.28), calls=%async_computation | async-start | bytes 131072 | tf_op jit(solution)/shard_map/all_to_all | solution.py:271
  19.2 3.1 %collective-permute-start = (f32[5,8,4,128]{3,2,1,0:T(4,128)}, f32[5,8,4,128]{3,2,1,0:T(4,128)S(1)}, u32[]{:S(2)}, u32[]{:S(2)}) collective-permute-start(f32[5,8,4,128]{3,2,1,0:T(4,128)} %get-tuple-element.12), channel_id=1, source_target_pairs={{0,16},{16,0},{32,48},{48,32},{64,80},{80,64},{96,112},{112,96},{1... | collective-permute-start | bytes 245768 | tf_op jit(solution)/shard_map/ppermute | solution.py:296
  22.3 2.8 %collective-permute-start.1 = (f32[5,8,4,128]{3,2,1,0:T(4,128)}, f32[5,8,4,128]{3,2,1,0:T(4,128)S(1)}, u32[]{:S(2)}, u32[]{:S(2)}) collective-permute-start(f32[5,8,4,128]{3,2,1,0:T(4,128)} %get-tuple-element.16), channel_id=1, source_target_pairs={{0,496},{16,32},{32,16},{48,64},{64,48},{80,96},{96,80},{112,128},... | collective-permute-start | bytes 245768 | tf_op jit(solution)/shard_map/ppermute | solution.py:295
  25.1 0.3 collective-permute-done.arrived.paired
  25.3 0.6 %prepare_rows.1.held = f32[15,32,8,128]{3,2,1,0:T(8,128)S(1)} custom-call(f32[5,8,4,128]{3,2,1,0:T(4,128)S(1)} %collective-permute-done.arrived.paired, f32[5,32,8,128]{3,2,1,0:T(8,128)S(1)} %get-tuple-element.13.kept), custom_call_target="tpu_custom_call" | custom-call | flops 4000000 | bytes 2600000 | tf_op jit(solution)/shard_map/prepare_rows/pallas_call | solution.py:299
  26.0 0.1 all-to-all-done
  26.0 0.1 reduce_max.9
  26.1 0.6 %broadcast_in_dim.4 = f32[8,1,128]{2,1,0:T(1,128)} broadcast(f32[128]{0:T(128)S(1)} %reduce_max.9), dimensions={2} | broadcast | bytes 4608 | tf_op jit(solution)/shard_map/broadcast_in_dim | solution.py:298
  26.7 6.6 %all-to-all-start.1 = ((f32[8,1,128]{2,1,0:T(1,128)}), f32[8,1,128]{2,1,0:T(1,128)S(1)}, u32[]{:S(2)}, u32[]{:S(2)}) async-start(f32[8,1,128]{2,1,0:T(1,128)} %broadcast_in_dim.4), calls=%async_computation.1 | async-start | bytes 8192 | tf_op jit(solution)/shard_map/all_to_all | solution.py:271
  33.3 0.0 collective-permute-done.1.other
  33.3 2.8 %all-to-all-done.1 = f32[8,1,128]{2,1,0:T(1,128)S(1)} async-done(((f32[8,1,128]{2,1,0:T(1,128)}), f32[8,1,128]{2,1,0:T(1,128)S(1)}, u32[]{:S(2)}, u32[]{:S(2)}) %all-to-all-start.1) | async-done | bytes 4128 | tf_op jit(solution)/shard_map/all_to_all | solution.py:271
  36.2 3.4 %plane_sweeps.1 = f32[16,10,8,128]{3,2,1,0:T(8,128)S(1)} custom-call(s32[1,1]{1,0:T(1,128)} %bitcast.odd, f32[8,128]{1,0:T(8,128)S(1)} %bitcast.23, f32[15,32,8,128]{3,2,1,0:T(8,128)S(1)} %prepare_rows.1.held, f32[5,8,4,128]{3,2,1,0:T(4,128)S(1)} %collective-permute-done.arrived.paired, f32[5,8,4,128]{3,2,1,0:T(4,128)S(1)} %collective-permute-done.1.other), custom_call_target="tpu_custom_call" | custom-call | tf_op jit(solution)/shard_map/plane_sweeps/pallas_call | solution.py:314
  39.5 14.1 %all_to_all.15.lines = f32[16,10,8,128]{3,2,1,0:T(8,128)S(1)} all-to-all(f32[16,10,8,128]{3,2,1,0:T(8,128)S(1)} %plane_sweeps.1), channel_id=1, replica_groups={{13,12,15,14,9,8,11,10,5,4,7,6,1,0,3,2},{29,28,31,30,25,24,27,26,21,20,..., dimensions={0} | all-to-all | bytes 1310720 | tf_op jit(solution)/shard_map/all_to_all | solution.py:324
  53.6 2.1 %column_sweep.1 = f32[5,16,16,128]{3,2,1,0:T(8,128)} custom-call(f32[8,128]{1,0:T(8,128)S(1)} %bitcast.24, f32[16,10,8,128]{3,2,1,0:T(8,128)S(1)} %all_to_all.15.lines), custom_call_target="tpu_custom_call" | custom-call | tf_op jit(solution)/shard_map/column_sweep/pallas_call | solution.py:325
Async XLA Ops:
  1.9 24.1 %all-to-all-start = ((f32[64,2,128]{2,1,0:T(2,128)}), f32[64,2,128]{2,1,0:T(2,128)S(1)}, u32[]{:S(2)}, u32[]{:S(2)}) async-start(f32[64,2,128]{2,1,0:T(2,128)} %bitcast.28), calls=%async_computation | async-start | bytes 131072 | tf_op jit(solution)/shard_map/all_to_all | solution.py:271
  19.2 6.1 %collective-permute-start = (f32[5,8,4,128]{3,2,1,0:T(4,128)}, f32[5,8,4,128]{3,2,1,0:T(4,128)S(1)}, u32[]{:S(2)}, u32[]{:S(2)}) collective-permute-start(f32[5,8,4,128]{3,2,1,0:T(4,128)} %get-tuple-element.12), channel_id=1, source_target_pairs={{0,16},{16,0},{32,48},{48,32},{64,80},{80,64},{96,112},{112,96},{1... | collective-permute-start | bytes 245768 | tf_op jit(solution)/shard_map/ppermute | solution.py:296
  22.3 11.1 %collective-permute-start.1 = (f32[5,8,4,128]{3,2,1,0:T(4,128)}, f32[5,8,4,128]{3,2,1,0:T(4,128)S(1)}, u32[]{:S(2)}, u32[]{:S(2)}) collective-permute-start(f32[5,8,4,128]{3,2,1,0:T(4,128)} %get-tuple-element.16), channel_id=1, source_target_pairs={{0,496},{16,32},{32,16},{48,64},{64,48},{80,96},{96,80},{112,128},... | collective-permute-start | bytes 245768 | tf_op jit(solution)/shard_map/ppermute | solution.py:295
  26.7 9.4 %all-to-all-start.1 = ((f32[8,1,128]{2,1,0:T(1,128)}), f32[8,1,128]{2,1,0:T(1,128)S(1)}, u32[]{:S(2)}, u32[]{:S(2)}) async-start(f32[8,1,128]{2,1,0:T(1,128)} %broadcast_in_dim.4), calls=%async_computation.1 | async-start | bytes 8192 | tf_op jit(solution)/shard_map/all_to_all | solution.py:271

commit v7 on v6

--- a/solution.py
+++ b/solution.py
@@ -244,20 +244,27 @@
     sweep_y(lines, out, star, speed, step)
 
 
-def column_kernel(top, lines, out):
+def column_kernel(top, lines, out, done, sems):
     step = step_of(top)
+
+    def ring(value, before, after):
+        return jnp.concatenate([value[DEPTH - before :], value, value[:after]], axis=0)
+
+    new = []
     for row in range(2):
         fields = [jnp.stack([lines[seat(z), 2 * index + row] for z in range(DEPTH)]) for index in range(5)]
         along, press, half_reach = primitives(fields[0], fields[1:4], fields[4], 2, step)
-
-        def ring(value, before, after):
-            return jnp.concatenate([value[DEPTH - before :], value, value[:after]], axis=0)
-
-        star_now, speed_now = interfaces(*(ring(value, 2, 3) for value in (fields[0], along, press, half_reach)))
-        new = remap([ring(f, 1, 1) for f in fields], 3, ring(star_now, 2, 1), ring(speed_now, 2, 1), step)
-        for index in range(5):
+        star, speed = interfaces(*(ring(value, 2, 3) for value in (fields[0], along, press, half_reach)))
+        new.append(remap([ring(f, 1, 1) for f in fields], 3, ring(star, 2, 1), ring(speed, 2, 1), step))
+    copies = []
+    for index in range(5):
+        for row in range(2):
             for z in range(DEPTH):
-                out[index, z, pl.ds(row, LINES, stride=2), :] = new[index][z]
+                done[index, z, pl.ds(row, LINES, stride=2), :] = new[row][index][z]
+        copies.append(pltpu.make_async_copy(done.at[index], out.at[index], sems.at[index]))
+        copies[-1].start()
+    for copy in copies:
+        copy.wait()
 
 
 def tiled(array):
@@ -326,7 +333,11 @@
         column_kernel,
         out_shape=jax.ShapeDtypeStruct((5, DEPTH, 2 * LINES, LANES), F32),
         in_specs=[vmem, vmem],
-        out_specs=vmem,
+        out_specs=pl.BlockSpec(memory_space=pl.ANY),
+        scratch_shapes=[
+            pltpu.VMEM((5, DEPTH, 2 * LINES, LANES), F32),
+            pltpu.SemaphoreType.DMA((5,)),
+        ],
         compiler_params=wide,
         name="column_sweep",
     )(top, lines)

time: 56.1 us -> 56 us (level)
  no operation moved by 1% of the time
where the time goes in v7:
time: 56 us; the launch traced here: 55.7 us
  starting transfers between devices  29.7 us (53%)
  blocking collectives  14.1 us (25%)
  Pallas kernels  7.96 us (14%)
  waiting for transfers between devices  3.18 us (6%)
  local copies, waits for them, and re-layouts  0.6 us (1%)
    all_to_all x2, starting transfers between devices, swap_speeds(): lax.all_to_all(speeds, axes, split_axis=0, concat_axis=0, tiled=True, axi...  23.9 us
    all_to_all x1, blocking collectives, local(): lax.all_to_all(lines, COL, split_axis=0, concat_axis=0, tiled=True, axis_...  14.1 us
    pallas_call x1, Pallas kernels, local(): pl.pallas_call(plane_kernel, out_shape=sent_shape, in_specs=[smem] + [vme...  3.36 us
    ppermute x1, starting transfers between devices, local(): paired = lax.ppermute(paired, ROW, [(i, i ^ 1) for i in range(rows)])  3.08 us
    all_to_all x2, waiting for transfers between devices, swap_speeds(): lax.all_to_all(speeds, axes, split_axis=0, concat_axis=0, tiled=True, axi...  2.93 us
    ppermute x1, starting transfers between devices, local(): lax.ppermute(other, ROW, [(i, (i + i % 2 * 2 - 1) % rows) for i in range(...  2.79 us
    pallas_call x1, Pallas kernels, local(): pl.pallas_call(column_kernel, out_shape=jax.ShapeDtypeStruct((5, DEPTH, 2...  2.09 us
    pallas_call x1, Pallas kernels, local(): pl.pallas_call(survey_kernel, out_shape=(jax.ShapeDtypeStruct((far * 2, L...  1.89 us
  transfers between devices with their start and end apart: 4, of which 3 were waited for; matrix products, arithmetic and copies ran while one was open for 1% of the time, Pallas kernels for 1%

profile of v7, /device:TPU:1, one launch (start us, length us, event | category | flops | bytes accessed | tf_op | source)
XLA Modules:
  0.0 55.7 jit_solution(16533042575140057453)
XLA Ops:
  0.0 1.9 %survey.1 = (f32[128,128]{1,0:T(8,128)}, f32[5,8,4,128]{3,2,1,0:T(4,128)}, f32[5,8,4,128]{3,2,1,0:T(4,128)}, f32[5,32,8,128]{3,2,1,0:T(8,128)S(1)}) custom-call(s32[1,1]{1,0:T(1,128)} %bitcast.odd, f32[256,128]{1,0:T(8,128)} %bitcast.26, f32[3,256,128]{2,1,0:T(8,128)} %bitcast.25, f32[256,128]{1,0:T(8,128)} %bitcast.27), custom_call_target="tpu_custom_call" | custom-call | tf_op jit(solution)/shard_map/survey/pallas_call | solution.py:295
  1.9 17.3 %all-to-all-start = ((f32[64,2,128]{2,1,0:T(2,128)}), f32[64,2,128]{2,1,0:T(2,128)S(1)}, u32[]{:S(2)}, u32[]{:S(2)}) async-start(f32[64,2,128]{2,1,0:T(2,128)} %bitcast.28), calls=%async_computation | async-start | bytes 131072 | tf_op jit(solution)/shard_map/all_to_all | solution.py:278
  19.2 3.1 %collective-permute-start = (f32[5,8,4,128]{3,2,1,0:T(4,128)}, f32[5,8,4,128]{3,2,1,0:T(4,128)S(1)}, u32[]{:S(2)}, u32[]{:S(2)}) collective-permute-start(f32[5,8,4,128]{3,2,1,0:T(4,128)} %get-tuple-element.12), channel_id=1, source_target_pairs={{0,16},{16,0},{32,48},{48,32},{64,80},{80,64},{96,112},{112,96},{1... | collective-permute-start | bytes 245768 | tf_op jit(solution)/shard_map/ppermute | solution.py:303
  22.3 2.8 %collective-permute-start.1 = (f32[5,8,4,128]{3,2,1,0:T(4,128)}, f32[5,8,4,128]{3,2,1,0:T(4,128)S(1)}, u32[]{:S(2)}, u32[]{:S(2)}) collective-permute-start(f32[5,8,4,128]{3,2,1,0:T(4,128)} %get-tuple-element.16), channel_id=1, source_target_pairs={{0,496},{16,32},{32,16},{48,64},{64,48},{80,96},{96,80},{112,128},... | collective-permute-start | bytes 245768 | tf_op jit(solution)/shard_map/ppermute | solution.py:302
  25.1 0.3 collective-permute-done.arrived.paired
  25.3 0.6 %prepare_rows.1.held = f32[15,32,8,128]{3,2,1,0:T(8,128)S(1)} custom-call(f32[5,8,4,128]{3,2,1,0:T(4,128)S(1)} %collective-permute-done.arrived.paired, f32[5,32,8,128]{3,2,1,0:T(8,128)S(1)} %get-tuple-element.13.kept), custom_call_target="tpu_custom_call" | custom-call | flops 4000000 | bytes 2600000 | tf_op jit(solution)/shard_map/prepare_rows/pallas_call | solution.py:306
  26.0 0.1 all-to-all-done
  26.0 0.1 reduce_max.9
  26.1 0.6 %broadcast_in_dim.4 = f32[8,1,128]{2,1,0:T(1,128)} broadcast(f32[128]{0:T(128)S(1)} %reduce_max.9), dimensions={2} | broadcast | bytes 4608 | tf_op jit(solution)/shard_map/broadcast_in_dim | solution.py:305
  26.7 6.6 %all-to-all-start.1 = ((f32[8,1,128]{2,1,0:T(1,128)}), f32[8,1,128]{2,1,0:T(1,128)S(1)}, u32[]{:S(2)}, u32[]{:S(2)}) async-start(f32[8,1,128]{2,1,0:T(1,128)} %broadcast_in_dim.4), calls=%async_computation.1 | async-start | bytes 8192 | tf_op jit(solution)/shard_map/all_to_all | solution.py:278
  33.3 0.0 collective-permute-done.1.other
  33.3 2.8 %all-to-all-done.1 = f32[8,1,128]{2,1,0:T(1,128)S(1)} async-done(((f32[8,1,128]{2,1,0:T(1,128)}), f32[8,1,128]{2,1,0:T(1,128)S(1)}, u32[]{:S(2)}, u32[]{:S(2)}) %all-to-all-start.1) | async-done | bytes 4128 | tf_op jit(solution)/shard_map/all_to_all | solution.py:278
  36.2 3.4 %plane_sweeps.1 = f32[16,10,8,128]{3,2,1,0:T(8,128)S(1)} custom-call(s32[1,1]{1,0:T(1,128)} %bitcast.odd, f32[8,128]{1,0:T(8,128)S(1)} %bitcast.23, f32[15,32,8,128]{3,2,1,0:T(8,128)S(1)} %prepare_rows.1.held, f32[5,8,4,128]{3,2,1,0:T(4,128)S(1)} %collective-permute-done.arrived.paired, f32[5,8,4,128]{3,2,1,0:T(4,128)S(1)} %collective-permute-done.1.other), custom_call_target="tpu_custom_call" | custom-call | tf_op jit(solution)/shard_map/plane_sweeps/pallas_call | solution.py:321
  39.5 14.1 %all_to_all.15.lines = f32[16,10,8,128]{3,2,1,0:T(8,128)S(1)} all-to-all(f32[16,10,8,128]{3,2,1,0:T(8,128)S(1)} %plane_sweeps.1), channel_id=1, replica_groups={{13,12,15,14,9,8,11,10,5,4,7,6,1,0,3,2},{29,28,31,30,25,24,27,26,21,20,..., dimensions={0} | all-to-all | bytes 1310720 | tf_op jit(solution)/shard_map/all_to_all | solution.py:331
  53.6 2.1 %column_sweep.1 = f32[5,16,16,128]{3,2,1,0:T(8,128)} custom-call(f32[8,128]{1,0:T(8,128)S(1)} %bitcast.24, f32[16,10,8,128]{3,2,1,0:T(8,128)S(1)} %all_to_all.15.lines), custom_call_target="tpu_custom_call" | custom-call | tf_op jit(solution)/shard_map/column_sweep/pallas_call | solution.py:332
Async XLA Ops:
  1.9 24.1 %all-to-all-start = ((f32[64,2,128]{2,1,0:T(2,128)}), f32[64,2,128]{2,1,0:T(2,128)S(1)}, u32[]{:S(2)}, u32[]{:S(2)}) async-start(f32[64,2,128]{2,1,0:T(2,128)} %bitcast.28), calls=%async_computation | async-start | bytes 131072 | tf_op jit(solution)/shard_map/all_to_all | solution.py:278
  19.2 6.1 %collective-permute-start = (f32[5,8,4,128]{3,2,1,0:T(4,128)}, f32[5,8,4,128]{3,2,1,0:T(4,128)S(1)}, u32[]{:S(2)}, u32[]{:S(2)}) collective-permute-start(f32[5,8,4,128]{3,2,1,0:T(4,128)} %get-tuple-element.12), channel_id=1, source_target_pairs={{0,16},{16,0},{32,48},{48,32},{64,80},{80,64},{96,112},{112,96},{1... | collective-permute-start | bytes 245768 | tf_op jit(solution)/shard_map/ppermute | solution.py:303
  22.3 11.1 %collective-permute-start.1 = (f32[5,8,4,128]{3,2,1,0:T(4,128)}, f32[5,8,4,128]{3,2,1,0:T(4,128)S(1)}, u32[]{:S(2)}, u32[]{:S(2)}) collective-permute-start(f32[5,8,4,128]{3,2,1,0:T(4,128)} %get-tuple-element.16), channel_id=1, source_target_pairs={{0,496},{16,32},{32,16},{48,64},{64,48},{80,96},{96,80},{112,128},... | collective-permute-start | bytes 245768 | tf_op jit(solution)/shard_map/ppermute | solution.py:302
  26.7 9.4 %all-to-all-start.1 = ((f32[8,1,128]{2,1,0:T(1,128)}), f32[8,1,128]{2,1,0:T(1,128)S(1)}, u32[]{:S(2)}, u32[]{:S(2)}) async-start(f32[8,1,128]{2,1,0:T(1,128)} %broadcast_in_dim.4), calls=%async_computation.1 | async-start | bytes 8192 | tf_op jit(solution)/shard_map/all_to_all | solution.py:278
